TPU v7x, 512 devices: a whole 4x8x8 slice. The times are simulated.
512 devices in a mesh: scene: 8 (over x, core), img: 64 (over y, z).
Axes of the slice: x: 4, y: 8, z: 8, core: 2. Of those that a mesh axis runs over, the one named last changes fastest.
Arguments:
- tokens: bfloat16 [8, 64, 8, 768], P('scene', 'img'), may hold values from -6 to 6
- pair_list: int32 [8, 64, 16, 2], P('scene', 'img'), may hold values from 0 to 63, as said below
- pair_count: int32 [8, 64], P('scene', 'img'), may hold values from 8 to 16, as said below
- poses: float32 [8, 64, 12], P('scene'), may hold values from -1.5 to 1.5
- gain_query: float32 [768], replicated, may hold values from 0.3 to 3
- gain_kv: float32 [768], replicated, may hold values from 0.3 to 3
- w_query: bfloat16 [768, 384], P('scene'), may hold values from -0.21875 to 0.21875
- w_kv: bfloat16 [768, 768], P('scene'), may hold values from -0.21875 to 0.21875
- w_out: bfloat16 [384, 768], P('scene'), may hold values from -0.3125 to 0.3125
- w_head: bfloat16 [768, 1024], P('scene'), may hold values from -0.21875 to 0.21875
Outputs:
- joined_points: bfloat16 [8, 64, 3, 2048], P('scene', 'img')
- pose_grad: float32 [8, 64, 3], P('scene', 'img')
Inputs may be any that keep to these rules, and one draw needn't show every extreme that they name: `pair_list`: indices are images of the owner's scene group; the two images of a pair differ; among the 16 slots of one device no image appears more than 1 times, and some device names one image 1 times; slot 0 of device d names image d first. `pair_count`: each device uses 16 slots or 8 of them; in every scene group some device uses all 16 slots.
All inputs are finite; a program needn't handle non-finite values.
Results may differ from a plain program's by a relative error of at most 0.034.
Values may be sent and summed in bfloat16 or wider, within the bound.
A program may use at most 64 MiB of HBM per device.

v0:
```python
import jax
import jax.numpy as jnp
from jax import lax
from jax.sharding import PartitionSpec as P

D = 768
HEADS = 6
HEAD_DIM = 64
PIX = 256
TOK = 8


def layer_norm(values_in, gain_vec):
    values_in = values_in.astype(jnp.float32)
    centered = values_in - jnp.mean(values_in, axis=-1, keepdims=True)
    variance = jnp.mean(centered * centered, axis=-1, keepdims=True)
    return centered * lax.rsqrt(variance + 1e-05) * gain_vec


def decode_views(view_tokens, gain_query, gain_kv, w_query, w_kv, w_out):
    view_count = view_tokens.shape[0]
    flat_rows = view_tokens.reshape(view_count * TOK, D)
    normed = layer_norm(flat_rows, gain_query).astype(jnp.bfloat16)
    queries = jnp.dot(normed, w_query, preferred_element_type=jnp.float32).astype(jnp.bfloat16)
    normed = layer_norm(flat_rows, gain_kv).astype(jnp.bfloat16)
    key_value = jnp.dot(normed, w_kv, preferred_element_type=jnp.float32).astype(jnp.bfloat16)
    key_value = jnp.flip(key_value.reshape(view_count // 2, 2, TOK, 2 * HEADS * HEAD_DIM), axis=1)
    key_value = key_value.reshape(view_count, TOK, 2, HEADS, HEAD_DIM)
    queries = queries.reshape(view_count, TOK, HEADS, HEAD_DIM)
    scores = jnp.einsum(
        "vqhd,vkhd->vhqk", queries, key_value[:, :, 0], preferred_element_type=jnp.float32
    )
    scores = scores * HEAD_DIM ** (-0.5)
    weights = jax.nn.softmax(scores, axis=-1).astype(jnp.bfloat16)
    attended = jnp.einsum(
        "vhqk,vkhd->vqhd", weights, key_value[:, :, 1], preferred_element_type=jnp.float32
    )
    attended = attended.astype(jnp.bfloat16).reshape(view_count * TOK, HEADS * HEAD_DIM)
    projected = jnp.dot(attended, w_out, preferred_element_type=jnp.float32)
    return (flat_rows.astype(jnp.float32) + projected).astype(jnp.bfloat16)


def point_head(decoded, w_head, pose_rows, in_use):
    view_count = pose_rows.shape[0]
    raw_out = jnp.dot(decoded, w_head, preferred_element_type=jnp.float32).reshape(
        view_count, TOK, 4, PIX
    )
    raw_out = jnp.transpose(raw_out, (0, 2, 1, 3)).reshape(view_count, 4, TOK * PIX)
    confidence = (1.0 + jnp.exp(raw_out[:, 3])) * in_use[:, None]
    rotation = jnp.eye(3, dtype=jnp.float32) + pose_rows[:, :9].reshape(view_count, 3, 3)
    world_pts = jnp.einsum(
        "vij,vjp->vip", rotation, raw_out[:, :3], precision=lax.Precision.HIGHEST
    )
    return (confidence, world_pts + pose_rows[:, 9:, None])


def on_device(
    tokens, pair_list, pair_count, poses, gain_query, gain_kv, w_query, w_kv, w_out, w_head
):
    w_query, w_kv, w_out, w_head = (
        lax.all_gather(w_query, "scene", axis=0, tiled=True),
        lax.all_gather(w_kv, "scene", axis=0, tiled=True),
        lax.all_gather(w_out, "scene", axis=0, tiled=True),
        lax.all_gather(w_head, "scene", axis=0, tiled=True),
    )
    group_size = lax.axis_size("img")
    image_ids = jnp.arange(group_size, dtype=jnp.int32)
    pair_rows = pair_list[0, 0]
    pair_slots = pair_rows.shape[0]
    view_image = pair_rows.reshape(-1)
    view_total = view_image.shape[0]
    in_use = jnp.repeat((jnp.arange(pair_slots) < pair_count[0, 0]).astype(jnp.float32), 2)
    first_image = jnp.repeat(pair_rows[:, 0], 2)
    first_hot = (first_image[:, None] == image_ids[None, :]).astype(jnp.float32)
    pose_table = poses[0]
    pose_rows = jnp.dot(first_hot, pose_table, precision=lax.Precision.HIGHEST)
    piece = lax.all_gather(tokens, "img", axis=1, tiled=True)
    piece_rows = piece.shape[1]
    chooser = (view_image[:, None] == jnp.arange(piece_rows)[None, :]).astype(jnp.bfloat16)
    flat_piece = piece.reshape(piece_rows, TOK * D)
    view_tokens = jnp.dot(chooser, flat_piece, preferred_element_type=jnp.float32).astype(
        jnp.bfloat16
    )
    decoded = decode_views(
        view_tokens.reshape(view_total, TOK, D), gain_query, gain_kv, w_query, w_kv, w_out
    )
    confidence, world_pts = point_head(decoded, w_head, pose_rows, in_use)
    image_hot = (view_image[:, None] == image_ids[None, :]).astype(jnp.float32)
    weighted_pts = confidence[:, None] * world_pts
    numerator = jnp.einsum("vi,vcp->icp", image_hot, weighted_pts, precision=lax.Precision.HIGHEST)
    denominator = jnp.einsum("vi,vp->ip", image_hot, confidence, precision=lax.Precision.HIGHEST)[
        :, None
    ]
    numerator, denominator = (
        lax.all_to_all(numerator, "img", split_axis=0, concat_axis=0, tiled=True),
        lax.all_to_all(denominator, "img", split_axis=0, concat_axis=0, tiled=True),
    )
    joined = (jnp.sum(numerator, axis=0) / jnp.sum(denominator, axis=0)).astype(jnp.bfloat16)
    piece = lax.all_gather(joined[None], "img", axis=0, tiled=True)
    piece_rows = piece.shape[0]
    chooser = (view_image[:, None] == jnp.arange(piece_rows)[None, :]).astype(jnp.bfloat16)
    flat_piece = piece.reshape(piece_rows, 3 * TOK * PIX)
    targets = jnp.dot(chooser, flat_piece, preferred_element_type=jnp.float32).astype(jnp.bfloat16)
    targets = targets.reshape(view_total, 3, TOK * PIX).astype(jnp.float32)
    residual_sum = jnp.sum(weighted_pts, axis=2) - jnp.sum(confidence[:, None] * targets, axis=2)
    gradient_part = jnp.einsum(
        "vi,vc->ic", first_hot, residual_sum, precision=lax.Precision.HIGHEST
    )
    gradient = lax.psum_scatter(gradient_part, "img", scatter_dimension=0, tiled=True) * (
        2.0 / (TOK * PIX)
    )
    return (joined.reshape(1, 1, 3, TOK * PIX), gradient.reshape(1, 1, 3))


def solution(mesh):
    return jax.shard_map(
        on_device,
        mesh=mesh,
        in_specs=(
            P("scene", "img", None, None),
            P("scene", "img", None, None),
            P("scene", "img"),
            P("scene", None, None),
            P(),
            P(),
            P("scene", None),
            P("scene", None),
            P("scene", None),
            P("scene", None),
        ),
        out_specs=(P("scene", "img", None, None), P("scene", "img", None)),
        check_vma=False,
    )
```

profile of v0, /device:TPU:6, one launch (start us, length us, event | category | flops | bytes accessed | tf_op | source)
XLA Modules:
  0.0 532.1 jit_solution(15758662708525127742)
XLA Ops:
  7.2 0.7 all-gather.3.cloned.1.call-update
  7.9 0.7 all-gather.5.cloned.1.call-update
  8.6 0.8 copy.27
  9.5 57.5 %all_gather.18 = bf16[1,64,8,768]{3,2,0,1:T(8,128)(2,1)S(1)} all-gather(bf16[1,1,8,768]{3,2,0,1:T(8,128)(2,1)} %bitcast.79), channel_id=1, replica_groups=mesh['scene'=8,'img'=64] {'img'}, dimensions={1}, use_global_device_ids=true | all-gather | bytes 798720 | tf_op jit(solution)/shard_map/all_gather | solution.py:77
  68.0 0.4 copy-done
  68.4 13.2 %all_gather.20 = bf16[768,384]{1,0:T(8,128)(2,1)S(1)} all-gather(bf16[96,384]{1,0:T(8,128)(2,1)S(1)} %copy-done), channel_id=1, replica_groups=mesh['scene'=8,'img'=64] {'scene'}, dimensions={0}, use_global_device_ids=true | all-gather | bytes 663552 | tf_op jit(solution)/shard_map/all_gather | solution.py:61
  81.5 0.4 convolution_convert_fusion.4
  83.1 13.2 %all_gather.21 = bf16[384,768]{1,0:T(8,128)(2,1)S(1)} all-gather(bf16[48,768]{1,0:T(8,128)(2,1)S(1)} %copy-done.1), channel_id=1, replica_groups=mesh['scene'=8,'img'=64] {'scene'}, dimensions={0}, use_global_device_ids=true | all-gather | bytes 663552 | tf_op jit(solution)/shard_map/all_gather | solution.py:63
  96.3 1.8 convolution_convert_fusion.2
  98.1 0.7 reshape.143
  98.8 1.1 fusion.46
  99.9 0.7 fusion.47
  100.9 1.6 fusion.7
  103.0 2.2 fusion.8
  105.2 0.5 reshape.147
  105.7 0.5 broadcast_multiply_fusion
  106.3 0.5 convolution_bitcast_fusion
  106.8 1.3 copy.38
  108.1 8.6 %all-to-all-start.1 = ((f32[64,1,2048]{2,1,0:T(1,128)}), f32[64,1,2048]{2,1,0:T(1,128)S(1)}, u32[]{:S(2)}, u32[]{:S(2)}) async-start(f32[64,1,2048]{2,1,0:T(1,128)} %copy.38), calls=%async_computation.1 | async-start | bytes 1048576 | tf_op jit(solution)/shard_map/all_to_all | solution.py:96
  117.5 2.1 fusion.50
  119.6 1.3 fusion.10
  120.9 2.4 copy.37
  123.3 12.7 %all-to-all-done.1 = f32[64,1,2048]{2,1,0:T(1,128)S(1)} async-done(((f32[64,1,2048]{2,1,0:T(1,128)}), f32[64,1,2048]{2,1,0:T(1,128)S(1)}, u32[]{:S(2)}, u32[]{:S(2)}) %all-to-all-start.1) | async-done | bytes 524320 | tf_op jit(solution)/shard_map/all_to_all | solution.py:96
  136.0 5.9 %all-to-all-start = ((f32[64,3,2048]{2,1,0:T(4,128)}), f32[64,3,2048]{2,1,0:T(4,128)S(1)}, u32[]{:S(2)}, u32[]{:S(2)}) async-start(f32[64,3,2048]{2,1,0:T(4,128)} %copy.37), calls=%async_computation | async-start | bytes 4194304 | tf_op jit(solution)/shard_map/all_to_all | solution.py:95
  141.9 1.3 dynamic-slice
  143.5 49.7 %all-to-all-done = f32[64,3,2048]{2,1,0:T(4,128)S(1)} async-done(((f32[64,3,2048]{2,1,0:T(4,128)}), f32[64,3,2048]{2,1,0:T(4,128)S(1)}, u32[]{:S(2)}, u32[]{:S(2)}) %all-to-all-start) | async-done | bytes 1572896 | tf_op jit(solution)/shard_map/all_to_all | solution.py:95
  193.5 0.6 fusion.25
  194.1 51.2 %all_gather.23 = bf16[64,3,2048]{2,1,0:T(4,128)(2,1)S(1)} all-gather(bf16[1,3,2048]{2,1,0:T(4,128)(2,1)S(1)} %fusion.26), channel_id=1, replica_groups=mesh['scene'=8,'img'=64] {'img'}, dimensions={0}, use_global_device_ids=true | all-gather | bytes 798720 | tf_op jit(solution)/shard_map/all_gather | solution.py:99
  245.4 0.6 copy.46
  246.3 0.6 reshape.152
  247.5 276.7 %all-reduce = f32[64,3]{1,0:T(8,128)S(1)} all-reduce(f32[64,3]{1,0:T(8,128)S(1)} %fusion.27), channel_id=2, replica_groups=mesh['scene'=8,'img'=64] {'img'}, use_global_device_ids=true, to_apply=%region_8.9.clone | all-reduce | flops 192 | bytes 1536
  524.2 1.1 fusion.41
  (47 shorter events, 4.7 us)
Async XLA Ops:
  7.2 89.1 %all-gather.3.cloned.1.call-start = ((), (), s32[]{:S(2)}) async-start(), calls=%async_computation.2 | async-start | bytes 1327104 | tf_op jit(solution)/shard_map/all_gather | solution.py:62
  7.9 95.1 %all-gather.5.cloned.1.call-start = ((), (), s32[]{:S(2)}) async-start(), calls=%async_computation.3 | async-start | bytes 1769472 | tf_op jit(solution)/shard_map/all_gather | solution.py:64
  67.5 0.9 copy-start
  67.5 14.0 %copy-start.2 = (f32[768]{0:T(1024)S(1)}, f32[768]{0:T(1024)}, u32[]{:S(2)}) copy-start(f32[768]{0:T(1024)} %param.14) | copy-start | bytes 9220
  68.0 15.1 %copy-start.1 = (bf16[48,768]{1,0:T(8,128)(2,1)S(1)}, bf16[48,768]{1,0:T(8,128)(2,1)}, u32[]{:S(2)}) copy-start(bf16[48,768]{1,0:T(8,128)(2,1)} %param.18) | copy-start | bytes 221188
  81.5 14.8 %copy-start.3 = (f32[768]{0:T(1024)S(1)}, f32[768]{0:T(1024)}, u32[]{:S(2)}) copy-start(f32[768]{0:T(1024)} %param.15) | copy-start | bytes 9220
  106.3 10.5 %copy-start.4 = (s32[1,1,16,2]{2,3,1,0:T(2,128)S(1)}, s32[1,1,16,2]{2,3,1,0:T(2,128)}, u32[]{:S(2)}) copy-start(s32[1,1,16,2]{2,3,1,0:T(2,128)} %param.11) | copy-start | bytes 388
  106.3 10.7 %copy-start.5 = (f32[1,64,12]{1,0,2:T(1,128)S(1)}, f32[1,64,12]{1,0,2:T(1,128)}, u32[]{:S(2)}) copy-start(f32[1,64,12]{1,0,2:T(1,128)} %param.13) | copy-start | bytes 9220
  108.1 27.9 %all-to-all-start.1 = ((f32[64,1,2048]{2,1,0:T(1,128)}), f32[64,1,2048]{2,1,0:T(1,128)S(1)}, u32[]{:S(2)}, u32[]{:S(2)}) async-start(f32[64,1,2048]{2,1,0:T(1,128)} %copy.38), calls=%async_computation.1 | async-start | bytes 1048576 | tf_op jit(solution)/shard_map/all_to_all | solution.py:96
  136.0 57.1 %all-to-all-start = ((f32[64,3,2048]{2,1,0:T(4,128)}), f32[64,3,2048]{2,1,0:T(4,128)S(1)}, u32[]{:S(2)}, u32[]{:S(2)}) async-start(f32[64,3,2048]{2,1,0:T(4,128)} %copy.37), calls=%async_computation | async-start | bytes 4194304 | tf_op jit(solution)/shard_map/all_to_all | solution.py:95
Sparse Core Ops, SparseCore 0:
  10.1 32.2 all-gather.2
  44.5 29.6 all-gather.4
where the time goes:
time: 533 us; the launch traced here: 532 us
  blocking collectives  412 us (77%)
  waiting for transfers between devices  63.7 us (12%)
  between operations  15 us (3%)
  starting transfers between devices  14.6 us (3%)
  matrix products  12 us (2%)
  local copies, waits for them, and re-layouts  11.4 us (2%)
    unnamed x1, blocking collectives  277 us
    all_gather x1, blocking collectives, on_device(): piece = lax.all_gather(tokens, 'img', axis=1, tiled=True)  57.5 us
    all_gather x1, blocking collectives, on_device(): piece = lax.all_gather(joined[None], 'img', axis=0, tiled=True)  51.2 us
    all_to_all x1, waiting for transfers between devices, on_device(): lax.all_to_all(numerator, 'img', split_axis=0, concat_axis=0, tiled=True)  49.7 us
    all_gather x1, blocking collectives, on_device(): lax.all_gather(w_out, 'scene', axis=0, tiled=True)  13.2 us
    all_gather x1, blocking collectives, on_device(): lax.all_gather(w_query, 'scene', axis=0, tiled=True)  13.2 us
    all_to_all x1, waiting for transfers between devices, on_device(): lax.all_to_all(denominator, 'img', split_axis=0, concat_axis=0, tiled=True)  12.7 us
  transfers between devices with their start and end apart: 4, of which 2 were waited for; matrix products, arithmetic and copies ran while one was open for 3% of the time, Pallas kernels for 0%

commit v1 on v0

v1 whole, which is shorter than its diff:
```python
import jax
import jax.numpy as jnp
from jax import lax
from jax.experimental import pallas as pl
from jax.experimental.pallas import tpu as pltpu
from jax.sharding import PartitionSpec as P

D = 768
HALF = D // 2
HEADS = 6
HEAD_DIM = 64
WIDTH = HEADS * HEAD_DIM
PIX = 256
TOK = 8
SLOTS = 16
SIDE = 8
IMAGES = SIDE * SIDE
RING = 4
GROUP = 16
ROWS = GROUP * TOK
BF16 = jnp.bfloat16
F32 = jnp.float32

SHARD = (96, 96, 48, 96)
SPLIT = (48, 48, 32, 48)


def dot(a, b):
    return jnp.dot(a, b, preferred_element_type=F32)


def dot_nt(a, b):
    return lax.dot_general(a, b, (((1,), (1,)), ((), ())), preferred_element_type=F32)


def iota(shape, dim):
    return lax.broadcasted_iota(jnp.int32, shape, dim)


def kernel(
    tok_ref, pair_ref, count_ref, pose_ref, gq_ref, gk_ref, wkv_in, wq_in, wo_in, wh_in,
    joined_ref, grad_ref,
    wkv, wq, wo, wh, nkg, info_in, info, y_s, c_s, z_s, coef_s, hg, hin, tin,
    w_send, w_recv, n_send, n_recv, i_send, i_recv, g_send, g_recv, own_sem,
):
    scene, img = lax.axis_index("scene"), lax.axis_index("img")
    x, core = scene // 2, scene % 2
    yy, zz = img // SIDE, img % SIDE
    outer = (1 - core) * yy + core * zz
    inner = (1 - core) * zz + core * yy
    mypos = outer * SIDE + inner

    def img_of(o, n):
        return (1 - core) * (o * SIDE + n) + core * (n * SIDE + o)

    def turn(v, by):
        return lax.rem(v + by, SIDE)

    right = (lax.rem(x + 1, RING) * 2 + core, img)
    left = (lax.rem(x + 3, RING) * 2 + core, img)
    twin = (x * 2 + 1 - core, img)
    in_peer = [None] + [(scene, img_of(outer, turn(inner, k))) for k in range(1, SIDE)]
    out_peer = [None] + [(scene, img_of(turn(outer, k), inner)) for k in range(1, SIDE)]

    barrier = pltpu.get_barrier_semaphore()
    peers = [right, left, twin] + in_peer[1:] + out_peer[1:]
    for peer in peers:
        pl.semaphore_signal(barrier, inc=1, device_id=peer, device_id_type=pl.DeviceIdType.MESH)

    def remote(src, dst, send, recv, peer):
        return pltpu.make_async_remote_copy(
            src_ref=src, dst_ref=dst, send_sem=send, recv_sem=recv,
            device_id=peer, device_id_type=pl.DeviceIdType.MESH,
        )

    xt = tok_ref[0, 0].astype(F32)
    centered = xt - jnp.mean(xt, axis=-1, keepdims=True)
    normed = centered * lax.rsqrt(jnp.mean(centered * centered, axis=-1, keepdims=True) + 1e-05)
    nq = (normed * gq_ref[...].reshape(1, D)).astype(BF16)
    nk = normed * gk_ref[...].reshape(1, D)
    nkg[mypos] = jnp.concatenate([nk[:, :HALF], nk[:, HALF:]], axis=0).astype(BF16)

    lane = iota((1, 128), 1)
    count = count_ref[0, 0]
    row = jnp.full((1, 128), -1.0, F32)
    for k in range(SLOTS):
        first = pair_ref[0, 0, k, 0].astype(F32)
        second = pair_ref[0, 0, k, 1].astype(F32)
        live = (lane < 64) & (k >= count)
        hit = (lane == k) | (lane == 80 + k)
        row = jnp.where(hit & ~live, first, row)
        hit = (lane == 16 + k) | (lane == 64 + k)
        row = jnp.where(hit & ~live, second, row)
    tile = jnp.where(iota((SIDE, 128), 0) == inner, jnp.broadcast_to(row, (SIDE, 128)), 0.0)
    info_in[inner] = tile

    pl.semaphore_wait(barrier, len(peers))

    started = []
    for k in range(1, SIDE):
        copy = remote(nkg.at[mypos], nkg.at[mypos], n_send.at[0, k], n_recv.at[0, k], in_peer[k])
        copy.start()
        started.append(copy)
        copy = remote(info_in.at[inner], info_in.at[inner], i_send.at[0, k], i_recv.at[0, k], in_peer[k])
        copy.start()
        started.append(copy)

    sources = (wkv_in, wq_in, wo_in, wh_in)
    gathered = (wkv, wq, wo, wh)

    def part(a, s, lo=0, size=None):
        size = SHARD[a] if size is None else size
        return gathered[a].at[pl.ds(pl.multiple_of(s * SHARD[a] + lo, 16), size)]

    def shard_of(dx, dc):
        return lax.rem(x + dx + RING, RING) * 2 + (1 - core if dc else core)

    local = []
    for a in range(4):
        for n, peer in enumerate((right, left, twin)):
            copy = remote(sources[a], part(a, scene), w_send.at[a, n], w_recv.at[a, n], peer)
            copy.start()
            started.append(copy)
        copy = pltpu.make_async_copy(sources[a], part(a, scene), own_sem.at[a])
        copy.start()
        local.append(copy)

    for k in range(1, SIDE):
        src = outer * SIDE + turn(inner, SIDE - k)
        remote(nkg.at[src], nkg.at[src], n_send.at[0, k], n_recv.at[0, k], in_peer[k]).wait_recv()
        slot = turn(inner, SIDE - k)
        remote(info_in.at[slot], info_in.at[slot], i_send.at[0, k], i_recv.at[0, k], in_peer[k]).wait_recv()
    total = info_in[0]
    for k in range(1, SIDE):
        total = total + info_in[k]
    info[outer] = total
    block = nkg.at[pl.ds(outer * SIDE, SIDE)]
    for k in range(1, SIDE):
        copy = remote(block, block, n_send.at[1, k], n_recv.at[1, k], out_peer[k])
        copy.start()
        started.append(copy)
        copy = remote(info.at[outer], info.at[outer], i_send.at[1, k], i_recv.at[1, k], out_peer[k])
        copy.start()
        started.append(copy)

    def got(a, n, ref):
        remote(ref, ref, w_send.at[a, n], w_recv.at[a, n], twin).wait_recv()

    def send(a, n, ref, peer):
        copy = remote(ref, ref, w_send.at[a, n], w_recv.at[a, n], peer)
        copy.start()
        started.append(copy)

    for a in range(4):
        near = part(a, shard_of(-1, 0))
        got(a, 0, near)
        send(a, 3, part(a, shard_of(-1, 0), 0, SPLIT[a]), right)
        send(a, 5, near, twin)
        near = part(a, shard_of(1, 0))
        got(a, 1, near)
        send(a, 4, part(a, shard_of(1, 0), SPLIT[a], SHARD[a] - SPLIT[a]), left)
        send(a, 6, near, twin)
    for a in range(4):
        far = part(a, shard_of(2, 0), 0, SPLIT[a])
        got(a, 3, far)
        send(a, 7, far, twin)
        far = part(a, shard_of(2, 0), SPLIT[a], SHARD[a] - SPLIT[a])
        got(a, 4, far)
        send(a, 8, far, twin)

    for k in range(1, SIDE):
        slot = turn(outer, SIDE - k)
        remote(info.at[slot], info.at[slot], i_send.at[1, k], i_recv.at[1, k], out_peer[k]).wait_recv()
    table = info[...].reshape(IMAGES, 128)
    partner = pltpu.roll(table, 64, 1) + 1.0
    lanes = iota((IMAGES, 128), 1)
    match = table == img.astype(F32)
    ones = jnp.ones((SIDE, 128), F32)
    as_first = dot_nt(ones, jnp.where(match & (lanes < 16), partner, 0.0))
    as_second = dot_nt(ones, jnp.where(match & (lanes >= 16) & (lanes < 32), partner, 0.0))
    pos_row = iota((IMAGES, IMAGES), 0)
    pos_col = iota((IMAGES, IMAGES), 1)
    image_at = (1 - core) * pos_row + core * (pos_row % SIDE * SIDE + pos_row // SIDE)
    name = (image_at + 1).astype(F32)
    m1 = jnp.sum(jnp.where(as_first[0:1] == name, 1.0, 0.0), axis=1, keepdims=True)
    m2 = jnp.sum(jnp.where(as_second[0:1] == name, 1.0, 0.0), axis=1, keepdims=True)
    pose = jnp.concatenate([pose_ref[0], jnp.ones((IMAGES, 1), F32), jnp.zeros((IMAGES, 115), F32)], axis=1)
    pose = pose + jnp.where((lanes == 0) | (lanes == 4) | (lanes == 8), 1.0, 0.0)
    pose = jnp.dot(
        jnp.where(image_at == pos_col, 1.0, 0.0), pose,
        precision=lax.Precision.HIGHEST, preferred_element_type=F32,
    )
    mine = jnp.sum(jnp.where(iota((IMAGES, 128), 0) == mypos, pose, 0.0), axis=0, keepdims=True)
    coef = m1 * mine + m2 * pose
    coef_s[...] = jnp.broadcast_to(coef[:, None, :], (IMAGES, TOK, 128)).reshape(IMAGES * TOK, 128)

    for k in range(1, SIDE):
        src = nkg.at[pl.ds(turn(outer, SIDE - k) * SIDE, SIDE)]
        remote(src, src, n_send.at[1, k], n_recv.at[1, k], out_peer[k]).wait_recv()

    def finish(a):
        local[a].wait()
        got(a, 2, part(a, shard_of(0, 1)))
        got(a, 5, part(a, shard_of(-1, 1)))
        got(a, 6, part(a, shard_of(1, 1)))
        got(a, 7, part(a, shard_of(2, 1), 0, SPLIT[a]))
        got(a, 8, part(a, shard_of(2, 1), SPLIT[a], SHARD[a] - SPLIT[a]))

    finish(0)
    finish(1)
    q = dot(nq, wq[...]).astype(BF16).astype(F32) * HEAD_DIM ** (-0.5)
    qbig = jnp.concatenate([q] * HEADS, axis=0)
    own_head = iota((HEADS * TOK, WIDTH), 0) // TOK == iota((HEADS * TOK, WIDTH), 1) // HEAD_DIM
    qbig = jnp.where(own_head, qbig, 0.0).astype(BF16)
    finish(2)
    same = iota((ROWS, ROWS), 0) // TOK == iota((ROWS, ROWS), 1) // TOK
    head_of = iota((ROWS, WIDTH), 1) // HEAD_DIM
    x_tile = jnp.concatenate([xt] * GROUP, axis=0)

    def attend(g, carry):
        block = nkg[pl.ds(g * GROUP, GROUP)].astype(F32)
        low = block[:, :TOK].reshape(ROWS, HALF).astype(BF16)
        high = block[:, TOK:].reshape(ROWS, HALF).astype(BF16)
        kv = dot(low, wkv[:HALF]) + dot(high, wkv[HALF:])
        keys = kv[:, :WIDTH].astype(BF16)
        values = kv[:, WIDTH:].astype(BF16).astype(F32)
        scores = dot_nt(keys, qbig).reshape(GROUP, TOK, HEADS * TOK)
        e = jnp.exp(scores - jnp.max(scores, axis=1, keepdims=True))
        attn = (e / jnp.sum(e, axis=1, keepdims=True)).reshape(ROWS, HEADS * TOK)
        turned = attn.T
        spread = []
        for h in range(HEADS):
            piece = jnp.concatenate([turned[h * TOK:(h + 1) * TOK]] * GROUP, axis=0)
            spread.append(jnp.where(same, piece, 0.0).astype(BF16))
        split = [jnp.where(head_of == h, values, 0.0).astype(BF16) for h in range(HEADS)]
        o = dot(jnp.concatenate(spread, axis=1), jnp.concatenate(split, axis=0)).astype(BF16)
        y_s[pl.ds(pl.multiple_of(g * ROWS, ROWS), ROWS)] = (x_tile + dot(o, wo[...])).astype(BF16)
        return carry

    lax.fori_loop(0, IMAGES // GROUP, attend, 0)
    finish(3)

    def points(g, carry):
        rows = pl.ds(pl.multiple_of(g * ROWS, ROWS), ROWS)
        r = dot(y_s[rows], wh[...])
        cf = coef_s[rows]
        conf = 1.0 + jnp.exp(jnp.where(cf[:, 12:13] > 0.0, r[:, 3 * PIX:], 0.0))
        pts = [conf * r[:, k * PIX:(k + 1) * PIX] for k in range(3)]
        c_s[rows] = conf
        for n, value in enumerate(pts + [conf]):
            z_s[n, rows] = value[:, :128] + value[:, 128:]
        new = []
        for k in range(3):
            w = cf[:, 9 + k:10 + k] * conf
            for m in range(3):
                w = w + cf[:, 3 * k + m:3 * k + m + 1] * pts[m]
            new.append(carry[k] + jnp.sum(w.reshape(GROUP, TOK, PIX), axis=0))
        w = cf[:, 12:13] * conf
        new.append(carry[3] + jnp.sum(w.reshape(GROUP, TOK, PIX), axis=0))
        return tuple(new)

    zero = jnp.zeros((TOK, PIX), F32)
    sums = lax.fori_loop(0, IMAGES // GROUP, points, (zero,) * 4)
    joined = [(sums[k] / sums[3]).astype(BF16).astype(F32) for k in range(3)]
    joined_rows = [jnp.concatenate([j[t:t + 1] for t in range(TOK)], axis=1) for j in joined]
    joined_ref[0, 0] = jnp.concatenate(joined_rows, axis=0).astype(BF16)

    conf = c_s[...]
    coarse = conf.astype(BF16)
    fine = (conf - coarse.astype(F32)).astype(BF16)
    target = jnp.concatenate(joined, axis=0).astype(BF16)
    cross = dot_nt(coarse, target) + dot_nt(fine, target)
    agree = iota((IMAGES * TOK, 3 * TOK), 0) % TOK == iota((IMAGES * TOK, 3 * TOK), 1) % TOK
    cross = jnp.sum(jnp.where(agree, cross, 0.0).reshape(IMAGES, TOK, 3 * TOK), axis=1)
    channel = iota((IMAGES, 3 * TOK), 1) // TOK
    met = [jnp.sum(jnp.where(channel == k, cross, 0.0), axis=1, keepdims=True) for k in range(3)]
    total = [
        jnp.sum(jnp.sum(z_s[n].reshape(IMAGES, TOK, 128), axis=1), axis=1, keepdims=True)
        for n in range(4)
    ]
    sent = jnp.zeros((IMAGES, 128), F32)
    kept = jnp.zeros((1, 128), F32)
    for k in range(3):
        theirs = pose[:, 9 + k:10 + k] * total[3] - met[k]
        ours = mine[:, 9 + k:10 + k] * total[3] - met[k]
        for m in range(3):
            theirs = theirs + pose[:, 3 * k + m:3 * k + m + 1] * total[m]
            ours = ours + mine[:, 3 * k + m:3 * k + m + 1] * total[m]
        sent = jnp.where(lanes == k, m2 * theirs, sent)
        kept = jnp.where(lane == k, jnp.sum(m1 * ours, axis=0, keepdims=True), kept)
    hg[...] = sent.reshape(SIDE, SIDE, 128)

    for k in range(1, SIDE):
        to = turn(outer, k)
        copy = remote(hg.at[to], hin.at[outer], g_send.at[0, k], g_recv.at[0, k], out_peer[k])
        copy.start()
        started.append(copy)
    hin[outer] = hg[outer]
    for k in range(1, SIDE):
        slot = hin.at[turn(outer, SIDE - k)]
        remote(slot, slot, g_send.at[0, k], g_recv.at[0, k], out_peer[k]).wait_recv()
    tin[inner] = jnp.sum(hin[...], axis=0)
    for k in range(1, SIDE):
        slot = tin.at[inner]
        copy = remote(slot, slot, g_send.at[1, k], g_recv.at[1, k], in_peer[k])
        copy.start()
        started.append(copy)
    for k in range(1, SIDE):
        slot = tin.at[turn(inner, SIDE - k)]
        remote(slot, slot, g_send.at[1, k], g_recv.at[1, k], in_peer[k]).wait_recv()
    tiles = jnp.sum(tin[...], axis=0)
    row = jnp.sum(jnp.where(iota((SIDE, 128), 0) == inner, tiles, 0.0), axis=0, keepdims=True)
    grad_ref[0] = ((row + kept) * (2.0 / (TOK * PIX)))[:, :3]

    for copy in started:
        copy.wait_send()


def on_device(
    tokens, pair_list, pair_count, poses, gain_query, gain_kv, w_query, w_kv, w_out, w_head
):
    vmem = pl.BlockSpec(memory_space=pltpu.VMEM)
    smem = pl.BlockSpec(memory_space=pltpu.SMEM)
    hbm = pl.BlockSpec(memory_space=pl.ANY)
    dma = pltpu.SemaphoreType.DMA
    return pl.pallas_call(
        kernel,
        out_shape=(
            jax.ShapeDtypeStruct((1, 1, 3, TOK * PIX), BF16),
            jax.ShapeDtypeStruct((1, 1, 3), F32),
        ),
        in_specs=[vmem, smem, smem, vmem, vmem, vmem, hbm, hbm, hbm, hbm],
        out_specs=(vmem, vmem),
        scratch_shapes=[
            pltpu.VMEM((D, D), BF16),
            pltpu.VMEM((D, WIDTH), BF16),
            pltpu.VMEM((WIDTH, D), BF16),
            pltpu.VMEM((D, 4 * PIX), BF16),
            pltpu.VMEM((IMAGES, 2 * TOK, HALF), BF16),
            pltpu.VMEM((SIDE, SIDE, 128), F32),
            pltpu.VMEM((SIDE, SIDE, 128), F32),
            pltpu.VMEM((IMAGES * TOK, D), BF16),
            pltpu.VMEM((IMAGES * TOK, PIX), F32),
            pltpu.VMEM((4, IMAGES * TOK, 128), F32),
            pltpu.VMEM((IMAGES * TOK, 128), F32),
            pltpu.VMEM((SIDE, SIDE, 128), F32),
            pltpu.VMEM((SIDE, SIDE, 128), F32),
            pltpu.VMEM((SIDE, SIDE, 128), F32),
            dma((4, 9)),
            dma((4, 9)),
            dma((2, SIDE)),
            dma((2, SIDE)),
            dma((2, SIDE)),
            dma((2, SIDE)),
            dma((2, SIDE)),
            dma((2, SIDE)),
            dma((4,)),
        ],
        compiler_params=pltpu.CompilerParams(
            collective_id=0, has_side_effects=True, vmem_limit_bytes=40 * 1024 * 1024
        ),
    )(tokens, pair_list, pair_count, poses, gain_query, gain_kv, w_kv, w_query, w_out, w_head)


def solution(mesh):
    return jax.shard_map(
        on_device,
        mesh=mesh,
        in_specs=(
            P("scene", "img", None, None),
            P("scene", "img", None, None),
            P("scene", "img"),
            P("scene", None, None),
            P(),
            P(),
            P("scene", None),
            P("scene", None),
            P("scene", None),
            P("scene", None),
        ),
        out_specs=(P("scene", "img", None, None), P("scene", "img", None)),
        check_vma=False,
    )
```

time: 533 us -> 58.7 us (0.11)
  the two profiles are of different devices: /device:TPU:6 before, /device:TPU:1 now
where the time goes in v1:
time: 58.7 us; the launch traced here: 58.3 us
  Pallas kernels  50.8 us (87%)
  local copies, waits for them, and re-layouts  6.19 us (11%)
  between operations  1.32 us (2%)
    pallas_call x1, Pallas kernels, on_device(): pl.pallas_call(kernel, out_shape=(jax.ShapeDtypeStruct((1, 1, 3, TOK * PI...  50.8 us
    unnamed x20, local copies, waits for them, and re-layouts  6.19 us

profile of v1, /device:TPU:1, one launch (start us, length us, event | category | flops | bytes accessed | tf_op | source)
XLA Modules:
  0.0 58.3 jit_solution(16682948472108263795)
XLA Ops:
  0.6 0.0 copy-start.7
  1.3 0.8 %copy.12.pair_ref = s32[1,1,16,2]{3,2,1,0:T(8,128)S(1)} copy(s32[1,1,16,2]{2,3,1,0:T(2,128)} %param.11) | data formatting | bytes 256 | tf_op args[1]
  2.1 0.0 copy-done.7
  2.1 0.0 copy-start.4
  2.1 0.0 copy-start.5
  2.1 0.0 copy-start.6
  2.1 0.1 copy.13.pose_ref
  2.2 0.6 %copy-done.4 = bf16[1,1,8,768]{3,2,1,0:T(8,128)(2,1)S(1)} copy-done((bf16[1,1,8,768]{3,2,1,0:T(8,128)(2,1)S(1)}, bf16[1,1,8,768]{3,2,1,0:T(8,128)(2,1)}, u32[]{:S(2)}) %copy-start.4) | copy-done | bytes 12312
  2.8 0.0 copy-done.5
  2.8 0.0 copy-done.6
  2.8 0.0 copy-start
  2.8 0.9 %copy-done = bf16[96,1024]{1,0:T(8,128)(2,1)S(1)} copy-done((bf16[96,1024]{1,0:T(8,128)(2,1)S(1)}, bf16[96,1024]{1,0:T(8,128)(2,1)}, u32[]{:S(2)}) %copy-start) | copy-done | bytes 196632
  3.7 0.0 copy-start.1
  3.7 0.9 %copy-done.1 = bf16[96,768]{1,0:T(8,128)(2,1)S(1)} copy-done((bf16[96,768]{1,0:T(8,128)(2,1)S(1)}, bf16[96,768]{1,0:T(8,128)(2,1)}, u32[]{:S(2)}) %copy-start.1) | copy-done | bytes 147480
  4.6 0.0 copy-start.2
  4.6 0.9 %copy-done.2 = bf16[96,384]{1,0:T(8,128)(2,1)S(1)} copy-done((bf16[96,384]{1,0:T(8,128)(2,1)S(1)}, bf16[96,384]{1,0:T(8,128)(2,1)}, u32[]{:S(2)}) %copy-start.2) | copy-done | bytes 73752
  5.5 0.0 copy-start.3
  5.5 0.9 %copy-done.3 = bf16[48,768]{1,0:T(8,128)(2,1)S(1)} copy-done((bf16[48,768]{1,0:T(8,128)(2,1)S(1)}, bf16[48,768]{1,0:T(8,128)(2,1)}, u32[]{:S(2)}) %copy-start.3) | copy-done | bytes 73752
  6.4 50.8 %shard_map.113 = (bf16[1,1,3,2048]{3,2,1,0:T(4,128)(2,1)S(1)}, f32[1,1,3]{2,1,0:T(1,128)S(1)}) custom-call(bf16[1,1,8,768]{3,2,1,0:T(8,128)(2,1)S(1)} %copy-done.4, s32[1,1,16,2]{3,2,1,0:T(8,128)S(1)} %copy.12.pair_ref, s32[1,1]{1,0:T(1,128)S(6)} %copy.16.count_ref, f32[1,64,12]{2,1,0:T(8,128)S(1)} %copy.13.pose_ref, f32[768]{0:T(1024)S(1)} %copy-done.5, ...), custom_call_target="tpu_custom_call" | custom-call | tf_op jit(solution)/shard_map/pallas_call | solution.py:326
  57.2 0.6 %copy.17 = bf16[1,1,3,2048]{3,2,1,0:T(4,128)(2,1)} copy(bf16[1,1,3,2048]{3,2,1,0:T(4,128)(2,1)S(1)} %get-tuple-element.4) | data formatting | bytes 24576
  57.8 0.5 copy.18
Async XLA Ops:
  0.6 1.4 %copy-start.7 = (f32[1,64,12]{1,0,2:T(1,128)S(1)}, f32[1,64,12]{1,0,2:T(1,128)}, u32[]{:S(2)}) copy-start(f32[1,64,12]{1,0,2:T(1,128)} %param.13) | copy-start | bytes 9220
  2.1 0.7 %copy-start.4 = (bf16[1,1,8,768]{3,2,1,0:T(8,128)(2,1)S(1)}, bf16[1,1,8,768]{3,2,1,0:T(8,128)(2,1)}, u32[]{:S(2)}) copy-start(bf16[1,1,8,768]{3,2,1,0:T(8,128)(2,1)} %tok_ref.1) | copy-start | bytes 36868
  2.1 0.7 %copy-start.5 = (f32[768]{0:T(1024)S(1)}, f32[768]{0:T(1024)}, u32[]{:S(2)}) copy-start(f32[768]{0:T(1024)} %gq_ref.1) | copy-start | bytes 9220
  2.1 0.7 %copy-start.6 = (f32[768]{0:T(1024)S(1)}, f32[768]{0:T(1024)}, u32[]{:S(2)}) copy-start(f32[768]{0:T(1024)} %gk_ref.1) | copy-start | bytes 9220
  2.8 0.9 %copy-start = (bf16[96,1024]{1,0:T(8,128)(2,1)S(1)}, bf16[96,1024]{1,0:T(8,128)(2,1)}, u32[]{:S(2)}) copy-start(bf16[96,1024]{1,0:T(8,128)(2,1)} %wh_in.1) | copy-start | bytes 589828
  3.7 0.9 %copy-start.1 = (bf16[96,768]{1,0:T(8,128)(2,1)S(1)}, bf16[96,768]{1,0:T(8,128)(2,1)}, u32[]{:S(2)}) copy-start(bf16[96,768]{1,0:T(8,128)(2,1)} %wkv_in.1) | copy-start | bytes 442372
  4.6 0.9 %copy-start.2 = (bf16[96,384]{1,0:T(8,128)(2,1)S(1)}, bf16[96,384]{1,0:T(8,128)(2,1)}, u32[]{:S(2)}) copy-start(bf16[96,384]{1,0:T(8,128)(2,1)} %wq_in.1) | copy-start | bytes 221188
  5.5 0.9 %copy-start.3 = (bf16[48,768]{1,0:T(8,128)(2,1)S(1)}, bf16[48,768]{1,0:T(8,128)(2,1)}, u32[]{:S(2)}) copy-start(bf16[48,768]{1,0:T(8,128)(2,1)} %wo_in.1) | copy-start | bytes 221188

commit v2 on v1

v2 whole, which is shorter than its diff:
```python
import jax
import jax.numpy as jnp
from jax import lax
from jax.experimental import pallas as pl
from jax.experimental.pallas import tpu as pltpu
from jax.sharding import PartitionSpec as P

D = 768
HALF = D // 2
HEADS = 6
HEAD_DIM = 64
WIDTH = HEADS * HEAD_DIM
PIX = 256
TOK = 8
SLOTS = 16
SIDE = 8
IMAGES = SIDE * SIDE
RING = 4
GROUP = 16
ROWS = GROUP * TOK
BF16 = jnp.bfloat16
F32 = jnp.float32

PIECES = ((0, 0, 96, 48), (1, 0, 96, 48), (2, 0, 48, 32), (2, 48, 48, 16), (3, 0, 48, 32))
SHARD = (96, 96, 96, 48)
NEAR_FIRST = (1, 7, 2, 6, 3, 5, 4)


def dot(a, b):
    return jnp.dot(a, b, preferred_element_type=F32)


def dot_nt(a, b):
    return lax.dot_general(a, b, (((1,), (1,)), ((), ())), preferred_element_type=F32)


def iota(shape, dim):
    return lax.broadcasted_iota(jnp.int32, shape, dim)


def kernel(
    tok_in, pair_in, count_in, pose_in, gq_in, gk_in, wkv_in, wq_in, wo_in, wh_in,
    joined_ref, grad_ref,
    tok_s, pair_s, count_s, pose_s, gq_s, gk_s, wkv, wq, wo, wh, nkg, info_in, info, kv_s, o_s, c_s, z_s, coef_s, hg, hin,
    w_send, w_recv, n_send, n_recv, i_send, i_recv, g_send, g_recv, own_sem, in_sem,
):
    scene, img = lax.axis_index("scene"), lax.axis_index("img")
    x, core = scene // 2, scene % 2
    yy, zz = img // SIDE, img % SIDE
    outer = (1 - core) * yy + core * zz
    inner = (1 - core) * zz + core * yy
    mypos = outer * SIDE + inner

    def img_of(o, n):
        return (1 - core) * (o * SIDE + n) + core * (n * SIDE + o)

    def turn(v, by):
        return lax.rem(v + by, SIDE)

    right = (lax.rem(x + 1, RING) * 2 + core, img)
    left = (lax.rem(x + 3, RING) * 2 + core, img)
    twin = (x * 2 + 1 - core, img)
    in_peer = [None] + [(scene, img_of(outer, turn(inner, k))) for k in range(1, SIDE)]
    out_peer = [None] + [(scene, img_of(turn(outer, k), inner)) for k in range(1, SIDE)]

    loads = []
    small = ((tok_in, tok_s), (gq_in, gq_s), (gk_in, gk_s), (pair_in, pair_s), (count_in, count_s), (pose_in, pose_s))
    for n, (src, dst) in enumerate(small):
        copy = pltpu.make_async_copy(src, dst, in_sem.at[n])
        copy.start()
        loads.append(copy)
    barrier = pltpu.get_barrier_semaphore()
    peers = [right, left, twin] + in_peer[1:] + out_peer[1:]
    for peer in peers:
        pl.semaphore_signal(barrier, inc=1, device_id=peer, device_id_type=pl.DeviceIdType.MESH)

    def remote(src, dst, send, recv, peer):
        return pltpu.make_async_remote_copy(
            src_ref=src, dst_ref=dst, send_sem=send, recv_sem=recv,
            device_id=peer, device_id_type=pl.DeviceIdType.MESH,
        )

    for copy in loads:
        copy.wait()
    xt = tok_s[0, 0].astype(F32)
    centered = xt - jnp.mean(xt, axis=-1, keepdims=True)
    normed = centered * lax.rsqrt(jnp.mean(centered * centered, axis=-1, keepdims=True) + 1e-05)
    nq = (normed * gq_s[...].reshape(1, D)).astype(BF16)
    nk = normed * gk_s[...].reshape(1, D)
    nkg[mypos] = jnp.concatenate([nk[:, :HALF], nk[:, HALF:]], axis=0).astype(BF16)

    lane = iota((1, 128), 1)
    first, second = pair_s[0, 0, 0:1].astype(F32), pair_s[0, 0, 1:2].astype(F32)
    live = iota((1, SLOTS), 1) < count_s[...]
    gap = jnp.full((1, 32), -1.0, F32)
    row = jnp.concatenate(
        [jnp.where(live, first, -1.0), jnp.where(live, second, -1.0), gap, second, first, gap], axis=1
    )
    tile = jnp.where(iota((SIDE, 128), 0) == inner, jnp.broadcast_to(row, (SIDE, 128)), 0.0)
    info_in[inner] = tile

    pl.semaphore_wait(barrier, len(peers))

    sources = (wkv_in, wq_in, wh_in, wo_in)
    gathered = (wkv, wq, wh, wo)

    def part(p, s, lo=0, size=None):
        a, first_row, rows, _ = PIECES[p]
        size = rows if size is None else size
        return gathered[a].at[pl.ds(pl.multiple_of(s * SHARD[a] + (first_row + lo), 16), size)]

    def shard_of(dx, dc):
        return lax.rem(x + dx + RING, RING) * 2 + (1 - core if dc else core)

    local = []

    def own(p):
        a, first_row, rows, _ = PIECES[p]
        src = sources[a].at[pl.ds(first_row, rows)]
        for n, peer in enumerate((right, left, twin)):
            copy = remote(src, part(p, scene), w_send.at[p, n], w_recv.at[p, n], peer)
            copy.start()
            started.append(copy)
        copy = pltpu.make_async_copy(src, part(p, scene), own_sem.at[p])
        copy.start()
        local.append(copy)

    def got(p, n, ref):
        remote(ref, ref, w_send.at[p, n], w_recv.at[p, n], twin).wait_recv()

    def send(p, n, ref, peer):
        copy = remote(ref, ref, w_send.at[p, n], w_recv.at[p, n], peer)
        copy.start()
        started.append(copy)

    def near(p):
        turn_at = PIECES[p][3]
        block = part(p, shard_of(-1, 0))
        got(p, 0, block)
        send(p, 3, part(p, shard_of(-1, 0), 0, turn_at), right)
        send(p, 5, block, twin)
        block = part(p, shard_of(1, 0))
        got(p, 1, block)
        send(p, 4, part(p, shard_of(1, 0), turn_at, PIECES[p][2] - turn_at), left)
        send(p, 6, block, twin)

    def far(p):
        turn_at = PIECES[p][3]
        block = part(p, shard_of(2, 0), 0, turn_at)
        got(p, 3, block)
        send(p, 7, block, twin)
        block = part(p, shard_of(2, 0), turn_at, PIECES[p][2] - turn_at)
        got(p, 4, block)
        send(p, 8, block, twin)

    def finish(p):
        turn_at = PIECES[p][3]
        local[p].wait()
        got(p, 2, part(p, shard_of(0, 1)))
        got(p, 5, part(p, shard_of(-1, 1)))
        got(p, 6, part(p, shard_of(1, 1)))
        got(p, 7, part(p, shard_of(2, 1), 0, turn_at))
        got(p, 8, part(p, shard_of(2, 1), turn_at, PIECES[p][2] - turn_at))

    started = []

    def tokens_out(ref, k):
        copy = remote(ref, ref, n_send.at[1, k], n_recv.at[1, k], out_peer[k])
        copy.start()

    own(0)
    mine_ref = nkg.at[mypos]
    for k in reversed(NEAR_FIRST):
        copy = remote(mine_ref, mine_ref, n_send.at[0, k], n_recv.at[0, k], in_peer[k])
        copy.start()
        started.append(copy)
    for k in reversed(NEAR_FIRST):
        slot = info_in.at[inner]
        copy = remote(slot, slot, i_send.at[0, k], i_recv.at[0, k], in_peer[k])
        copy.start()
        started.append(copy)
    for k in reversed(NEAR_FIRST):
        tokens_out(mine_ref, k)
    own(1)
    own(2)
    for k in NEAR_FIRST:
        arrived = nkg.at[outer * SIDE + turn(inner, SIDE - k)]
        remote(arrived, arrived, n_send.at[0, k], n_recv.at[0, k], in_peer[k]).wait_recv()
        for m in reversed(NEAR_FIRST):
            tokens_out(arrived, m)
    for k in NEAR_FIRST:
        slot = info_in.at[turn(inner, SIDE - k)]
        remote(slot, slot, i_send.at[0, k], i_recv.at[0, k], in_peer[k]).wait_recv()
    total = info_in[0]
    for k in range(1, SIDE):
        total = total + info_in[k]
    info[outer] = total
    for k in reversed(NEAR_FIRST):
        copy = remote(info.at[outer], info.at[outer], i_send.at[1, k], i_recv.at[1, k], out_peer[k])
        copy.start()
        started.append(copy)
    near(0)
    own(3)
    own(4)
    near(1)
    near(2)
    far(0)

    for k in range(1, SIDE):
        slot = turn(outer, SIDE - k)
        remote(info.at[slot], info.at[slot], i_send.at[1, k], i_recv.at[1, k], out_peer[k]).wait_recv()
    table = info[...].reshape(IMAGES, 128)
    partner = pltpu.roll(table, 64, 1) + 1.0
    lanes = iota((IMAGES, 128), 1)
    match = table == img.astype(F32)
    ones = jnp.ones((SIDE, 128), F32)
    as_first = dot_nt(ones, jnp.where(match & (lanes < 16), partner, 0.0))
    as_second = dot_nt(ones, jnp.where(match & (lanes >= 16) & (lanes < 32), partner, 0.0))
    pos_row = iota((IMAGES, IMAGES), 0)
    pos_col = iota((IMAGES, IMAGES), 1)
    image_at = (1 - core) * pos_row + core * (pos_row % SIDE * SIDE + pos_row // SIDE)
    name = (image_at + 1).astype(F32)
    m1 = jnp.sum(jnp.where(as_first[0:1] == name, 1.0, 0.0), axis=1, keepdims=True)
    m2 = jnp.sum(jnp.where(as_second[0:1] == name, 1.0, 0.0), axis=1, keepdims=True)
    pose = jnp.concatenate(
        [pose_s[:, 0], jnp.ones((1, IMAGES), F32), jnp.zeros((115, IMAGES), F32)], axis=0
    )
    number = iota((128, IMAGES), 0)
    pose = pose + jnp.where((number == 0) | (number == 4) | (number == 8), 1.0, 0.0)
    pose = lax.dot_general(
        jnp.where(image_at == pos_col, 1.0, 0.0), pose, (((1,), (1,)), ((), ())),
        precision=lax.Precision.HIGHEST, preferred_element_type=F32,
    )
    mine = jnp.sum(jnp.where(iota((IMAGES, 128), 0) == mypos, pose, 0.0), axis=0, keepdims=True)
    coef = m1 * mine + m2 * pose
    coef_s[...] = jnp.broadcast_to(coef[:, None, :], (IMAGES, TOK, 128)).reshape(IMAGES * TOK, 128)

    for k in range(1, SIDE):
        src = nkg.at[pl.ds(turn(outer, SIDE - k) * SIDE, SIDE)]
        remote(src, src, n_send.at[1, k], n_recv.at[1, k], out_peer[k]).wait_recv()

    finish(0)

    def keys_values(g, carry):
        block = nkg[pl.ds(g * GROUP, GROUP)].astype(F32)
        low = block[:, :TOK].reshape(ROWS, HALF).astype(BF16)
        high = block[:, TOK:].reshape(ROWS, HALF).astype(BF16)
        rows = pl.ds(pl.multiple_of(g * ROWS, ROWS), ROWS)
        kv_s[rows] = (dot(low, wkv[:HALF]) + dot(high, wkv[HALF:])).astype(BF16)
        return carry

    lax.fori_loop(0, IMAGES // GROUP, keys_values, 0)
    near(3)
    near(4)
    far(1)
    finish(1)
    q = dot(nq, wq[...]).astype(BF16).astype(F32) * HEAD_DIM ** (-0.5)
    qbig = jnp.concatenate([q] * HEADS, axis=0)
    own_head = iota((HEADS * TOK, WIDTH), 0) // TOK == iota((HEADS * TOK, WIDTH), 1) // HEAD_DIM
    qbig = jnp.where(own_head, qbig, 0.0).astype(BF16)
    same = iota((ROWS, ROWS), 0) // TOK == iota((ROWS, ROWS), 1) // TOK
    head_of = iota((ROWS, WIDTH), 1) // HEAD_DIM
    x_tile = jnp.concatenate([xt] * GROUP, axis=0)

    def attend(g, carry):
        rows = pl.ds(pl.multiple_of(g * ROWS, ROWS), ROWS)
        keys = kv_s[rows, :WIDTH]
        values = kv_s[rows, WIDTH:].astype(F32)
        scores = dot_nt(keys, qbig).reshape(GROUP, TOK, HEADS * TOK)
        e = jnp.exp(scores - jnp.max(scores, axis=1, keepdims=True))
        attn = (e / jnp.sum(e, axis=1, keepdims=True)).reshape(ROWS, HEADS * TOK)
        turned = attn.T
        spread = []
        for h in range(HEADS):
            piece = jnp.concatenate([turned[h * TOK:(h + 1) * TOK]] * GROUP, axis=0)
            spread.append(jnp.where(same, piece, 0.0).astype(BF16))
        split = [jnp.where(head_of == h, values, 0.0).astype(BF16) for h in range(HEADS)]
        o = dot(jnp.concatenate(spread, axis=1), jnp.concatenate(split, axis=0))
        o_s[rows] = o.astype(BF16)
        return carry

    lax.fori_loop(0, 2, attend, 0)
    far(2)
    lax.fori_loop(2, IMAGES // GROUP, attend, 0)
    far(3)
    far(4)
    finish(2)
    finish(3)
    finish(4)

    def points(g, carry):
        rows = pl.ds(pl.multiple_of(g * ROWS, ROWS), ROWS)
        y = (x_tile + dot(o_s[rows], wo[...])).astype(BF16)
        r = dot(y, wh[...])
        cf = coef_s[rows]
        conf = 1.0 + jnp.exp(jnp.where(cf[:, 12:13] > 0.0, r[:, 3 * PIX:], 0.0))
        pts = [conf * r[:, k * PIX:(k + 1) * PIX] for k in range(3)]
        c_s[rows] = conf
        for n, value in enumerate(pts + [conf]):
            z_s[n, rows] = value[:, :128] + value[:, 128:]
        new = []
        for k in range(3):
            w = cf[:, 9 + k:10 + k] * conf
            for m in range(3):
                w = w + cf[:, 3 * k + m:3 * k + m + 1] * pts[m]
            new.append(carry[k] + jnp.sum(w.reshape(GROUP, TOK, PIX), axis=0))
        w = cf[:, 12:13] * conf
        new.append(carry[3] + jnp.sum(w.reshape(GROUP, TOK, PIX), axis=0))
        return tuple(new)

    zero = jnp.zeros((TOK, PIX), F32)
    sums = lax.fori_loop(0, IMAGES // GROUP, points, (zero,) * 4)
    joined = [(sums[k] / sums[3]).astype(BF16).astype(F32) for k in range(3)]
    joined_rows = [jnp.concatenate([j[t:t + 1] for t in range(TOK)], axis=1) for j in joined]
    joined_ref[0, 0] = jnp.concatenate(joined_rows, axis=0).astype(BF16)

    conf = c_s[...]
    coarse = conf.astype(BF16)
    fine = (conf - coarse.astype(F32)).astype(BF16)
    target = jnp.concatenate(joined, axis=0).astype(BF16)
    cross = dot_nt(coarse, target) + dot_nt(fine, target)
    agree = iota((IMAGES * TOK, 3 * TOK), 0) % TOK == iota((IMAGES * TOK, 3 * TOK), 1) % TOK
    cross = jnp.sum(jnp.where(agree, cross, 0.0).reshape(IMAGES, TOK, 3 * TOK), axis=1)
    channel = iota((IMAGES, 3 * TOK), 1) // TOK
    met = [jnp.sum(jnp.where(channel == k, cross, 0.0), axis=1, keepdims=True) for k in range(3)]
    total = [
        jnp.sum(jnp.sum(z_s[n].reshape(IMAGES, TOK, 128), axis=1), axis=1, keepdims=True)
        for n in range(4)
    ]
    sent = jnp.zeros((IMAGES, 128), F32)
    kept = jnp.zeros((1, 128), F32)
    for k in range(3):
        theirs = pose[:, 9 + k:10 + k] * total[3] - met[k]
        ours = mine[:, 9 + k:10 + k] * total[3] - met[k]
        for m in range(3):
            theirs = theirs + pose[:, 3 * k + m:3 * k + m + 1] * total[m]
            ours = ours + mine[:, 3 * k + m:3 * k + m + 1] * total[m]
        sent = jnp.where(lanes == k, m2 * theirs, sent)
        kept = jnp.where(lane == k, jnp.sum(m1 * ours, axis=0, keepdims=True), kept)
    hg[...] = sent.reshape(IMAGES, 1, 128)

    def give(n, carry):
        o, i = turn(outer, n // SIDE), turn(inner, n % SIDE)
        remote(hg.at[o * SIDE + i], hin.at[mypos], g_send.at[0], g_recv.at[0], (scene, img_of(o, i))).start()
        return carry

    lax.fori_loop(36, IMAGES, give, 0)
    lax.fori_loop(1, 36, give, 0)
    hin[mypos] = jnp.zeros((1, 128), F32)
    most = hin.at[pl.ds(0, IMAGES - 1)]
    exchange = remote(most, most, g_send.at[0], g_recv.at[0], twin)
    exchange.wait_recv()
    row = jnp.sum(hin[...], axis=0)
    grad_ref[0] = ((row + kept) * (2.0 / (TOK * PIX)))[:, :3]

    exchange.wait_send()
    all_tokens = nkg.at[pl.ds(outer * SIDE, SIDE)]
    for k in range(1, SIDE):
        remote(all_tokens, all_tokens, n_send.at[1, k], n_recv.at[1, k], out_peer[k]).wait_send()
    for copy in started:
        copy.wait_send()


def on_device(
    tokens, pair_list, pair_count, poses, gain_query, gain_kv, w_query, w_kv, w_out, w_head
):
    vmem = pl.BlockSpec(memory_space=pltpu.VMEM)
    hbm = pl.BlockSpec(memory_space=pltpu.HBM)
    dma = pltpu.SemaphoreType.DMA
    return pl.pallas_call(
        kernel,
        out_shape=(
            jax.ShapeDtypeStruct((1, 1, 3, TOK * PIX), BF16),
            jax.ShapeDtypeStruct((1, 1, 3), F32),
        ),
        in_specs=[hbm] * 10,
        out_specs=(vmem, vmem),
        scratch_shapes=[
            pltpu.VMEM((1, 1, TOK, D), BF16),
            pltpu.VMEM((1, 1, 2, SLOTS), jnp.int32),
            pltpu.VMEM((1, 1), jnp.int32),
            pltpu.VMEM((12, 1, IMAGES), F32),
            pltpu.VMEM((D,), F32),
            pltpu.VMEM((D,), F32),
            pltpu.VMEM((D, D), BF16),
            pltpu.VMEM((D, WIDTH), BF16),
            pltpu.VMEM((WIDTH, D), BF16),
            pltpu.VMEM((D, 4 * PIX), BF16),
            pltpu.VMEM((IMAGES, 2 * TOK, HALF), BF16),
            pltpu.VMEM((SIDE, SIDE, 128), F32),
            pltpu.VMEM((SIDE, SIDE, 128), F32),
            pltpu.VMEM((IMAGES * TOK, D), BF16),
            pltpu.VMEM((IMAGES * TOK, WIDTH), BF16),
            pltpu.VMEM((IMAGES * TOK, PIX), F32),
            pltpu.VMEM((4, IMAGES * TOK, 128), F32),
            pltpu.VMEM((IMAGES * TOK, 128), F32),
            pltpu.VMEM((IMAGES, 1, 128), F32),
            pltpu.VMEM((IMAGES, 1, 128), F32),
            dma((5, 9)),
            dma((5, 9)),
            dma((2, SIDE)),
            dma((2, SIDE)),
            dma((2, SIDE)),
            dma((2, SIDE)),
            dma((1,)),
            dma((1,)),
            dma((5,)),
            dma((6,)),
        ],
        compiler_params=pltpu.CompilerParams(
            collective_id=0, has_side_effects=True, vmem_limit_bytes=64 * 1024 * 1024
        ),
    )(
        tokens, jnp.swapaxes(pair_list, 2, 3), pair_count, jnp.transpose(poses, (2, 0, 1)),
        gain_query, gain_kv, w_kv, w_query, w_out, w_head,
    )


def solution(mesh):
    return jax.shard_map(
        on_device,
        mesh=mesh,
        in_specs=(
            P("scene", "img", None, None),
            P("scene", "img", None, None),
            P("scene", "img"),
            P("scene", None, None),
            P(),
            P(),
            P("scene", None),
            P("scene", None),
            P("scene", None),
            P("scene", None),
        ),
        out_specs=(P("scene", "img", None, None), P("scene", "img", None)),
        check_vma=False,
    )
```

time: 58.7 us -> 54 us (0.920)
  local copies, waits for them, and re-layouts: 6.19 us -> 1.84 us
    unnamed x20 -> x4, local copies, waits for them, and re-layouts: 6.19 us -> 1.84 us
where the time goes in v2:
time: 54 us; the launch traced here: 53.8 us
  Pallas kernels  50.6 us (94%)
  local copies, waits for them, and re-layouts  1.84 us (3%)
  between operations  1.3 us (2%)
    pallas_call x1, Pallas kernels, on_device(): pl.pallas_call(kernel, out_shape=(jax.ShapeDtypeStruct((1, 1, 3, TOK * PI...  50.6 us
    unnamed x4, local copies, waits for them, and re-layouts  1.84 us

profile of v2, /device:TPU:1, one launch (start us, length us, event | category | flops | bytes accessed | tf_op | source)
XLA Modules:
  0.0 53.8 jit_solution(9346914644926091895)
XLA Ops:
  1.3 50.6 %shard_map.113 = (bf16[1,1,3,2048]{3,2,1,0:T(4,128)(2,1)}, f32[1,1,3]{2,1,0:T(1,128)}) custom-call(bf16[1,1,8,768]{3,2,1,0:T(8,128)(2,1)} %tok_in.1, s32[1,1,2,16]{3,2,1,0:T(2,128)} %bitcast.3, s32[1,1]{1,0:T(1,128)S(6)} %copy.14.count_in, f32[12,1,64]{2,1,0:T(1,128)} %bitcast.2, f32[768]{0:T(1024)} %gq_in.1, f32[768]{0:T(1024)} %gk_in.1, ...), custom_call_target="tpu_custom_call" | custom-call | tf_op jit(solution)/shard_map/pallas_call | solution.py:370
  51.9 0.0 copy-start
  51.9 1.3 %copy.15 = bf16[1,1,3,2048]{3,2,1,0:T(4,128)(2,1)} copy(bf16[1,1,3,2048]{3,2,1,0:T(4,128)(2,1)} %get-tuple-element.4) | data formatting | bytes 24576
  53.3 0.0 copy-done
  53.3 0.5 copy.16
Async XLA Ops:
  51.9 1.3 %copy-start = (f32[1,1,3]{2,1,0:T(1,128)S(1)}, f32[1,1,3]{2,1,0:T(1,128)}, u32[]{:S(2)}) copy-start(f32[1,1,3]{2,1,0:T(1,128)} %get-tuple-element.5) | copy-start | bytes 40

commit v3 on v2

--- a/solution.py
+++ b/solution.py
@@ -18,12 +18,17 @@
 RING = 4
 GROUP = 16
 ROWS = GROUP * TOK
+WIDE = 32
+MANY = WIDE * TOK
 BF16 = jnp.bfloat16
 F32 = jnp.float32
 
-PIECES = ((0, 0, 96, 48), (1, 0, 96, 48), (2, 0, 48, 32), (2, 48, 48, 16), (3, 0, 48, 32))
-SHARD = (96, 96, 96, 48)
-NEAR_FIRST = (1, 7, 2, 6, 3, 5, 4)
+SHARD = 96
+MID = SHARD // 2
+OUT = 4 * PIX
+RING_ORDER = (0, 1, 7, 2, 6, 3, 5, 4)
+NEAR_FIRST = RING_ORDER[1:]
+EARLY = 3
 
 
 def dot(a, b):
@@ -41,15 +46,16 @@
 def kernel(
     tok_in, pair_in, count_in, pose_in, gq_in, gk_in, wkv_in, wq_in, wo_in, wh_in,
     joined_ref, grad_ref,
-    tok_s, pair_s, count_s, pose_s, gq_s, gk_s, wkv, wq, wo, wh, nkg, info_in, info, kv_s, o_s, c_s, z_s, coef_s, hg, hin,
-    w_send, w_recv, n_send, n_recv, i_send, i_recv, g_send, g_recv, own_sem, in_sem,
+    tok_s, pair_s, count_s, pose_s, gq_s, gk_s, wa, wb, wo, nkg, info_in, info, o_s, c_s, z_s, coef_s, hg, hin,
+    w_send, w_recv, n_send, n_recv, i_send, i_recv, g_send, g_recv, in_sem,
 ):
     scene, img = lax.axis_index("scene"), lax.axis_index("img")
     x, core = scene // 2, scene % 2
     yy, zz = img // SIDE, img % SIDE
     outer = (1 - core) * yy + core * zz
     inner = (1 - core) * zz + core * yy
-    mypos = outer * SIDE + inner
+    mypos = outer * SIDE
+    myname = outer * SIDE + inner
 
     def img_of(o, n):
         return (1 - core) * (o * SIDE + n) + core * (n * SIDE + o)
@@ -63,16 +69,27 @@
     in_peer = [None] + [(scene, img_of(outer, turn(inner, k))) for k in range(1, SIDE)]
     out_peer = [None] + [(scene, img_of(turn(outer, k), inner)) for k in range(1, SIDE)]
 
-    loads = []
-    small = ((tok_in, tok_s), (gq_in, gq_s), (gk_in, gk_s), (pair_in, pair_s), (count_in, count_s), (pose_in, pose_s))
-    for n, (src, dst) in enumerate(small):
-        copy = pltpu.make_async_copy(src, dst, in_sem.at[n])
-        copy.start()
-        loads.append(copy)
     barrier = pltpu.get_barrier_semaphore()
     peers = [right, left, twin] + in_peer[1:] + out_peer[1:]
     for peer in peers:
         pl.semaphore_signal(barrier, inc=1, device_id=peer, device_id_type=pl.DeviceIdType.MESH)
+
+    loads = []
+    row0 = pl.ds(pl.multiple_of(scene * SHARD, SHARD), SHARD)
+    top = pl.ds(pl.multiple_of(scene * SHARD, 16), MID)
+    bottom = pl.ds(pl.multiple_of(scene * SHARD + MID, 16), MID)
+    copies = (
+        (tok_in, tok_s), (gq_in, gq_s), (gk_in, gk_s), (pair_in, pair_s), (count_in, count_s),
+        (pose_in, pose_s),
+        (wq_in, wa.at[row0, pl.ds(0, WIDTH)]), (wkv_in, wa.at[row0, pl.ds(WIDTH, D)]),
+        (wh_in, wb.at[row0, pl.ds(0, OUT)]),
+        (wo_in.at[:, pl.ds(0, HALF)], wb.at[top, pl.ds(OUT, HALF)]),
+        (wo_in.at[:, pl.ds(HALF, HALF)], wb.at[bottom, pl.ds(OUT, HALF)]),
+    )
+    for n, (src, dst) in enumerate(copies):
+        copy = pltpu.make_async_copy(src, dst, in_sem.at[n])
+        copy.start()
+        loads.append(copy)
 
     def remote(src, dst, send, recv, peer):
         return pltpu.make_async_remote_copy(
@@ -80,7 +97,7 @@
             device_id=peer, device_id_type=pl.DeviceIdType.MESH,
         )
 
-    for copy in loads:
+    for copy in loads[:6]:
         copy.wait()
     xt = tok_s[0, 0].astype(F32)
     centered = xt - jnp.mean(xt, axis=-1, keepdims=True)
@@ -99,95 +116,80 @@
     tile = jnp.where(iota((SIDE, 128), 0) == inner, jnp.broadcast_to(row, (SIDE, 128)), 0.0)
     info_in[inner] = tile
 
+    for copy in loads[6:]:
+        copy.wait()
     pl.semaphore_wait(barrier, len(peers))
 
-    sources = (wkv_in, wq_in, wh_in, wo_in)
-    gathered = (wkv, wq, wh, wo)
-
-    def part(p, s, lo=0, size=None):
-        a, first_row, rows, _ = PIECES[p]
-        size = rows if size is None else size
-        return gathered[a].at[pl.ds(pl.multiple_of(s * SHARD[a] + (first_row + lo), 16), size)]
+    gathered = (wa, wb)
+
+    def part(p, s, lo=0, size=SHARD):
+        return gathered[p].at[pl.ds(pl.multiple_of(s * SHARD + lo, 16), size)]
 
     def shard_of(dx, dc):
         return lax.rem(x + dx + RING, RING) * 2 + (1 - core if dc else core)
 
-    local = []
-
-    def own(p):
-        a, first_row, rows, _ = PIECES[p]
-        src = sources[a].at[pl.ds(first_row, rows)]
-        for n, peer in enumerate((right, left, twin)):
-            copy = remote(src, part(p, scene), w_send.at[p, n], w_recv.at[p, n], peer)
-            copy.start()
-            started.append(copy)
-        copy = pltpu.make_async_copy(src, part(p, scene), own_sem.at[p])
-        copy.start()
-        local.append(copy)
-
-    def got(p, n, ref):
-        remote(ref, ref, w_send.at[p, n], w_recv.at[p, n], twin).wait_recv()
+    started = []
 
     def send(p, n, ref, peer):
         copy = remote(ref, ref, w_send.at[p, n], w_recv.at[p, n], peer)
         copy.start()
         started.append(copy)
 
+    def got(p, n, ref):
+        remote(ref, ref, w_send.at[p, n], w_recv.at[p, n], twin).wait_recv()
+
+    def own(p):
+        for n, peer in enumerate((right, left, twin)):
+            send(p, n, part(p, scene), peer)
+
     def near(p):
-        turn_at = PIECES[p][3]
-        block = part(p, shard_of(-1, 0))
-        got(p, 0, block)
-        send(p, 3, part(p, shard_of(-1, 0), 0, turn_at), right)
-        send(p, 5, block, twin)
-        block = part(p, shard_of(1, 0))
-        got(p, 1, block)
-        send(p, 4, part(p, shard_of(1, 0), turn_at, PIECES[p][2] - turn_at), left)
-        send(p, 6, block, twin)
+        got(p, 0, part(p, shard_of(-1, 0)))
+        send(p, 3, part(p, shard_of(-1, 0), 0, MID), right)
+        send(p, 5, part(p, shard_of(-1, 0)), twin)
+        got(p, 1, part(p, shard_of(1, 0)))
+        send(p, 4, part(p, shard_of(1, 0), MID, MID), left)
+        send(p, 6, part(p, shard_of(1, 0)), twin)
 
     def far(p):
-        turn_at = PIECES[p][3]
-        block = part(p, shard_of(2, 0), 0, turn_at)
-        got(p, 3, block)
-        send(p, 7, block, twin)
-        block = part(p, shard_of(2, 0), turn_at, PIECES[p][2] - turn_at)
-        got(p, 4, block)
-        send(p, 8, block, twin)
+        got(p, 3, part(p, shard_of(2, 0), 0, MID))
+        send(p, 7, part(p, shard_of(2, 0), 0, MID), twin)
+        got(p, 4, part(p, shard_of(2, 0), MID, MID))
+        send(p, 8, part(p, shard_of(2, 0), MID, MID), twin)
 
     def finish(p):
-        turn_at = PIECES[p][3]
-        local[p].wait()
         got(p, 2, part(p, shard_of(0, 1)))
         got(p, 5, part(p, shard_of(-1, 1)))
         got(p, 6, part(p, shard_of(1, 1)))
-        got(p, 7, part(p, shard_of(2, 1), 0, turn_at))
-        got(p, 8, part(p, shard_of(2, 1), turn_at, PIECES[p][2] - turn_at))
-
-    started = []
-
-    def tokens_out(ref, k):
-        copy = remote(ref, ref, n_send.at[1, k], n_recv.at[1, k], out_peer[k])
-        copy.start()
+        got(p, 7, part(p, shard_of(2, 1), 0, MID))
+        got(p, 8, part(p, shard_of(2, 1), MID, MID))
 
     own(0)
-    mine_ref = nkg.at[mypos]
     for k in reversed(NEAR_FIRST):
-        copy = remote(mine_ref, mine_ref, n_send.at[0, k], n_recv.at[0, k], in_peer[k])
+        slot = nkg.at[mypos + RING_ORDER.index(k)]
+        copy = remote(nkg.at[mypos], slot, n_send.at[0, k], n_recv.at[0, k], in_peer[k])
         copy.start()
         started.append(copy)
+    own(1)
     for k in reversed(NEAR_FIRST):
         slot = info_in.at[inner]
         copy = remote(slot, slot, i_send.at[0, k], i_recv.at[0, k], in_peer[k])
         copy.start()
         started.append(copy)
-    for k in reversed(NEAR_FIRST):
-        tokens_out(mine_ref, k)
-    own(1)
-    own(2)
-    for k in NEAR_FIRST:
-        arrived = nkg.at[outer * SIDE + turn(inner, SIDE - k)]
-        remote(arrived, arrived, n_send.at[0, k], n_recv.at[0, k], in_peer[k]).wait_recv()
-        for m in reversed(NEAR_FIRST):
-            tokens_out(arrived, m)
+
+    def arrive(k):
+        slot = nkg.at[mypos + RING_ORDER.index(k)]
+        remote(slot, slot, n_send.at[0, k], n_recv.at[0, k], in_peer[k]).wait_recv()
+
+    def pass_on(lo, size):
+        group = nkg.at[pl.ds(mypos + lo, size)]
+        for k in reversed(NEAR_FIRST):
+            remote(group, group, n_send.at[1, k], n_recv.at[1, k], out_peer[k]).start()
+
+    for k in RING_ORDER[1:EARLY]:
+        arrive(k)
+    pass_on(0, EARLY)
+    for k in RING_ORDER[EARLY:]:
+        arrive(k)
     for k in NEAR_FIRST:
         slot = info_in.at[turn(inner, SIDE - k)]
         remote(slot, slot, i_send.at[0, k], i_recv.at[0, k], in_peer[k]).wait_recv()
@@ -199,11 +201,9 @@
         copy = remote(info.at[outer], info.at[outer], i_send.at[1, k], i_recv.at[1, k], out_peer[k])
         copy.start()
         started.append(copy)
+    pass_on(EARLY, SIDE - EARLY)
     near(0)
-    own(3)
-    own(4)
     near(1)
-    near(2)
     far(0)
 
     for k in range(1, SIDE):
@@ -218,7 +218,10 @@
     as_second = dot_nt(ones, jnp.where(match & (lanes >= 16) & (lanes < 32), partner, 0.0))
     pos_row = iota((IMAGES, IMAGES), 0)
     pos_col = iota((IMAGES, IMAGES), 1)
-    image_at = (1 - core) * pos_row + core * (pos_row % SIDE * SIDE + pos_row // SIDE)
+    slot = pos_row % SIDE
+    back = (slot % 2) * ((slot + 1) // 2) + (1 - slot % 2) * (SIDE - slot // 2)
+    place = (inner - back + 2 * SIDE) % SIDE
+    image_at = (1 - core) * (pos_row // SIDE * SIDE + place) + core * (place * SIDE + pos_row // SIDE)
     name = (image_at + 1).astype(F32)
     m1 = jnp.sum(jnp.where(as_first[0:1] == name, 1.0, 0.0), axis=1, keepdims=True)
     m2 = jnp.sum(jnp.where(as_second[0:1] == name, 1.0, 0.0), axis=1, keepdims=True)
@@ -240,32 +243,22 @@
         remote(src, src, n_send.at[1, k], n_recv.at[1, k], out_peer[k]).wait_recv()
 
     finish(0)
-
-    def keys_values(g, carry):
-        block = nkg[pl.ds(g * GROUP, GROUP)].astype(F32)
-        low = block[:, :TOK].reshape(ROWS, HALF).astype(BF16)
-        high = block[:, TOK:].reshape(ROWS, HALF).astype(BF16)
-        rows = pl.ds(pl.multiple_of(g * ROWS, ROWS), ROWS)
-        kv_s[rows] = (dot(low, wkv[:HALF]) + dot(high, wkv[HALF:])).astype(BF16)
-        return carry
-
-    lax.fori_loop(0, IMAGES // GROUP, keys_values, 0)
-    near(3)
-    near(4)
-    far(1)
-    finish(1)
-    q = dot(nq, wq[...]).astype(BF16).astype(F32) * HEAD_DIM ** (-0.5)
+    q = dot(nq, wa[:, :WIDTH]).astype(BF16).astype(F32) * HEAD_DIM ** (-0.5)
     qbig = jnp.concatenate([q] * HEADS, axis=0)
     own_head = iota((HEADS * TOK, WIDTH), 0) // TOK == iota((HEADS * TOK, WIDTH), 1) // HEAD_DIM
     qbig = jnp.where(own_head, qbig, 0.0).astype(BF16)
     same = iota((ROWS, ROWS), 0) // TOK == iota((ROWS, ROWS), 1) // TOK
     head_of = iota((ROWS, WIDTH), 1) // HEAD_DIM
-    x_tile = jnp.concatenate([xt] * GROUP, axis=0)
+    x_tile = jnp.concatenate([xt] * WIDE, axis=0)
 
     def attend(g, carry):
         rows = pl.ds(pl.multiple_of(g * ROWS, ROWS), ROWS)
-        keys = kv_s[rows, :WIDTH]
-        values = kv_s[rows, WIDTH:].astype(F32)
+        block = nkg[pl.ds(g * GROUP, GROUP)].astype(F32)
+        low = block[:, :TOK].reshape(ROWS, HALF).astype(BF16)
+        high = block[:, TOK:].reshape(ROWS, HALF).astype(BF16)
+        kv = dot(low, wa[:HALF, WIDTH:]) + dot(high, wa[HALF:, WIDTH:])
+        keys = kv[:, :WIDTH].astype(BF16)
+        values = kv[:, WIDTH:].astype(BF16).astype(F32)
         scores = dot_nt(keys, qbig).reshape(GROUP, TOK, HEADS * TOK)
         e = jnp.exp(scores - jnp.max(scores, axis=1, keepdims=True))
         attn = (e / jnp.sum(e, axis=1, keepdims=True)).reshape(ROWS, HEADS * TOK)
@@ -280,18 +273,17 @@
         return carry
 
     lax.fori_loop(0, 2, attend, 0)
-    far(2)
+    far(1)
     lax.fori_loop(2, IMAGES // GROUP, attend, 0)
-    far(3)
-    far(4)
-    finish(2)
-    finish(3)
-    finish(4)
+    finish(1)
+    for s in range(D // SHARD):
+        wo[s * MID:(s + 1) * MID, :HALF] = wb[s * SHARD:s * SHARD + MID, OUT:]
+        wo[s * MID:(s + 1) * MID, HALF:] = wb[s * SHARD + MID:(s + 1) * SHARD, OUT:]
 
     def points(g, carry):
-        rows = pl.ds(pl.multiple_of(g * ROWS, ROWS), ROWS)
+        rows = pl.ds(pl.multiple_of(g * MANY, MANY), MANY)
         y = (x_tile + dot(o_s[rows], wo[...])).astype(BF16)
-        r = dot(y, wh[...])
+        r = dot(y, wb[:, :OUT])
         cf = coef_s[rows]
         conf = 1.0 + jnp.exp(jnp.where(cf[:, 12:13] > 0.0, r[:, 3 * PIX:], 0.0))
         pts = [conf * r[:, k * PIX:(k + 1) * PIX] for k in range(3)]
@@ -303,13 +295,13 @@
             w = cf[:, 9 + k:10 + k] * conf
             for m in range(3):
                 w = w + cf[:, 3 * k + m:3 * k + m + 1] * pts[m]
-            new.append(carry[k] + jnp.sum(w.reshape(GROUP, TOK, PIX), axis=0))
+            new.append(carry[k] + jnp.sum(w.reshape(WIDE, TOK, PIX), axis=0))
         w = cf[:, 12:13] * conf
-        new.append(carry[3] + jnp.sum(w.reshape(GROUP, TOK, PIX), axis=0))
+        new.append(carry[3] + jnp.sum(w.reshape(WIDE, TOK, PIX), axis=0))
         return tuple(new)
 
     zero = jnp.zeros((TOK, PIX), F32)
-    sums = lax.fori_loop(0, IMAGES // GROUP, points, (zero,) * 4)
+    sums = lax.fori_loop(0, IMAGES // WIDE, points, (zero,) * 4)
     joined = [(sums[k] / sums[3]).astype(BF16).astype(F32) for k in range(3)]
     joined_rows = [jnp.concatenate([j[t:t + 1] for t in range(TOK)], axis=1) for j in joined]
     joined_ref[0, 0] = jnp.concatenate(joined_rows, axis=0).astype(BF16)
@@ -339,26 +331,33 @@
         kept = jnp.where(lane == k, jnp.sum(m1 * ours, axis=0, keepdims=True), kept)
     hg[...] = sent.reshape(IMAGES, 1, 128)
 
-    def give(n, carry):
-        o, i = turn(outer, n // SIDE), turn(inner, n % SIDE)
-        remote(hg.at[o * SIDE + i], hin.at[mypos], g_send.at[0], g_recv.at[0], (scene, img_of(o, i))).start()
+    def give(o, k):
+        src = hg.at[o * SIDE + RING_ORDER.index((SIDE - k) % SIDE)]
+        peer = (scene, img_of(o, turn(inner, k)))
+        remote(src, hin.at[myname], g_send.at[0], g_recv.at[0], peer).start()
+
+    def give_row(n, carry):
+        u = SIDE - 1 - n
+        o = turn(outer, (u % 2) * ((u + 1) // 2) + (1 - u % 2) * (SIDE - u // 2))
+        for k in reversed(RING_ORDER):
+            give(o, k)
         return carry
 
-    lax.fori_loop(36, IMAGES, give, 0)
-    lax.fori_loop(1, 36, give, 0)
-    hin[mypos] = jnp.zeros((1, 128), F32)
+    lax.fori_loop(0, SIDE - 1, give_row, 0)
+    for k in reversed(NEAR_FIRST):
+        give(outer, k)
+    hin[myname] = jnp.zeros((1, 128), F32)
+    for copy in started:
+        copy.wait_send()
+    all_tokens = nkg.at[pl.ds(mypos, SIDE)]
+    for k in range(1, SIDE):
+        remote(all_tokens, all_tokens, n_send.at[1, k], n_recv.at[1, k], out_peer[k]).wait_send()
     most = hin.at[pl.ds(0, IMAGES - 1)]
     exchange = remote(most, most, g_send.at[0], g_recv.at[0], twin)
+    exchange.wait_send()
     exchange.wait_recv()
     row = jnp.sum(hin[...], axis=0)
     grad_ref[0] = ((row + kept) * (2.0 / (TOK * PIX)))[:, :3]
-
-    exchange.wait_send()
-    all_tokens = nkg.at[pl.ds(outer * SIDE, SIDE)]
-    for k in range(1, SIDE):
-        remote(all_tokens, all_tokens, n_send.at[1, k], n_recv.at[1, k], out_peer[k]).wait_send()
-    for copy in started:
-        copy.wait_send()
 
 
 def on_device(
@@ -382,30 +381,27 @@
             pltpu.VMEM((12, 1, IMAGES), F32),
             pltpu.VMEM((D,), F32),
             pltpu.VMEM((D,), F32),
-            pltpu.VMEM((D, D), BF16),
-            pltpu.VMEM((D, WIDTH), BF16),
+            pltpu.VMEM((D, WIDTH + D), BF16),
+            pltpu.VMEM((D, OUT + HALF), BF16),
             pltpu.VMEM((WIDTH, D), BF16),
-            pltpu.VMEM((D, 4 * PIX), BF16),
             pltpu.VMEM((IMAGES, 2 * TOK, HALF), BF16),
             pltpu.VMEM((SIDE, SIDE, 128), F32),
             pltpu.VMEM((SIDE, SIDE, 128), F32),
-            pltpu.VMEM((IMAGES * TOK, D), BF16),
             pltpu.VMEM((IMAGES * TOK, WIDTH), BF16),
             pltpu.VMEM((IMAGES * TOK, PIX), F32),
             pltpu.VMEM((4, IMAGES * TOK, 128), F32),
             pltpu.VMEM((IMAGES * TOK, 128), F32),
             pltpu.VMEM((IMAGES, 1, 128), F32),
             pltpu.VMEM((IMAGES, 1, 128), F32),
-            dma((5, 9)),
-            dma((5, 9)),
+            dma((2, 9)),
+            dma((2, 9)),
             dma((2, SIDE)),
             dma((2, SIDE)),
             dma((2, SIDE)),
             dma((2, SIDE)),
             dma((1,)),
             dma((1,)),
-            dma((5,)),
-            dma((6,)),
+            dma((11,)),
         ],
         compiler_params=pltpu.CompilerParams(
             collective_id=0, has_side_effects=True, vmem_limit_bytes=64 * 1024 * 1024

time: 54 us -> 50.5 us (0.935)
  Pallas kernels: 50.6 us -> 47.2 us
    pallas_call x1, Pallas kernels: 50.6 us -> 47.2 us  [on_device(): pl.pallas_call(kernel, out_shape=(jax.ShapeDtypeStruct((1, 1, 3, TOK * PI...]
where the time goes in v3:
time: 50.5 us; the launch traced here: 50.3 us
  Pallas kernels  47.2 us (93%)
  local copies, waits for them, and re-layouts  1.84 us (4%)
  between operations  1.3 us (3%)
    pallas_call x1, Pallas kernels, on_device(): pl.pallas_call(kernel, out_shape=(jax.ShapeDtypeStruct((1, 1, 3, TOK * PI...  47.2 us
    unnamed x4, local copies, waits for them, and re-layouts  1.84 us

profile of v3, /device:TPU:1, one launch (start us, length us, event | category | flops | bytes accessed | tf_op | source)
XLA Modules:
  0.0 50.3 jit_solution(16294358828910316715)
XLA Ops:
  1.3 47.2 %shard_map.113 = (bf16[1,1,3,2048]{3,2,1,0:T(4,128)(2,1)}, f32[1,1,3]{2,1,0:T(1,128)}) custom-call(bf16[1,1,8,768]{3,2,1,0:T(8,128)(2,1)} %tok_in.1, s32[1,1,2,16]{3,2,1,0:T(2,128)} %bitcast.3, s32[1,1]{1,0:T(1,128)S(6)} %copy.14.count_in, f32[12,1,64]{2,1,0:T(1,128)} %bitcast.2, f32[768]{0:T(1024)} %gq_in.1, f32[768]{0:T(1024)} %gk_in.1, ...), custom_call_target="tpu_custom_call" | custom-call | tf_op jit(solution)/shard_map/pallas_call | solution.py:369
  48.5 0.0 copy-start
  48.5 1.3 %copy.15 = bf16[1,1,3,2048]{3,2,1,0:T(4,128)(2,1)} copy(bf16[1,1,3,2048]{3,2,1,0:T(4,128)(2,1)} %get-tuple-element.4) | data formatting | bytes 24576
  49.8 0.0 copy-done
  49.8 0.5 %copy.16 = f32[1,1,3]{2,1,0:T(1,128)} copy(f32[1,1,3]{2,1,0:T(1,128)S(1)} %copy-done) | data formatting | bytes 24
Async XLA Ops:
  48.5 1.3 %copy-start = (f32[1,1,3]{2,1,0:T(1,128)S(1)}, f32[1,1,3]{2,1,0:T(1,128)}, u32[]{:S(2)}) copy-start(f32[1,1,3]{2,1,0:T(1,128)} %get-tuple-element.5) | copy-start | bytes 40

commit v4 on v3

--- a/solution.py
+++ b/solution.py
@@ -54,7 +54,6 @@
     yy, zz = img // SIDE, img % SIDE
     outer = (1 - core) * yy + core * zz
     inner = (1 - core) * zz + core * yy
-    mypos = outer * SIDE
     myname = outer * SIDE + inner
 
     def img_of(o, n):
@@ -63,16 +62,15 @@
     def turn(v, by):
         return lax.rem(v + by, SIDE)
 
-    right = (lax.rem(x + 1, RING) * 2 + core, img)
-    left = (lax.rem(x + 3, RING) * 2 + core, img)
+    way = 1 - 2 * core
+    right = (lax.rem(x + way + RING, RING) * 2 + core, img)
+    left = (lax.rem(x - way + RING, RING) * 2 + core, img)
     twin = (x * 2 + 1 - core, img)
     in_peer = [None] + [(scene, img_of(outer, turn(inner, k))) for k in range(1, SIDE)]
     out_peer = [None] + [(scene, img_of(turn(outer, k), inner)) for k in range(1, SIDE)]
 
     barrier = pltpu.get_barrier_semaphore()
-    peers = [right, left, twin] + in_peer[1:] + out_peer[1:]
-    for peer in peers:
-        pl.semaphore_signal(barrier, inc=1, device_id=peer, device_id_type=pl.DeviceIdType.MESH)
+    peers = [peer for k in reversed(NEAR_FIRST) for peer in (in_peer[k], out_peer[k])] + [right, left, twin]
 
     loads = []
     row0 = pl.ds(pl.multiple_of(scene * SHARD, SHARD), SHARD)
@@ -90,6 +88,8 @@
         copy = pltpu.make_async_copy(src, dst, in_sem.at[n])
         copy.start()
         loads.append(copy)
+    for peer in peers:
+        pl.semaphore_signal(barrier, inc=1, device_id=peer, device_id_type=pl.DeviceIdType.MESH)
 
     def remote(src, dst, send, recv, peer):
         return pltpu.make_async_remote_copy(
@@ -104,7 +104,7 @@
     normed = centered * lax.rsqrt(jnp.mean(centered * centered, axis=-1, keepdims=True) + 1e-05)
     nq = (normed * gq_s[...].reshape(1, D)).astype(BF16)
     nk = normed * gk_s[...].reshape(1, D)
-    nkg[mypos] = jnp.concatenate([nk[:, :HALF], nk[:, HALF:]], axis=0).astype(BF16)
+    nkg[0] = jnp.concatenate([nk[:, :HALF], nk[:, HALF:]], axis=0).astype(BF16)
 
     lane = iota((1, 128), 1)
     first, second = pair_s[0, 0, 0:1].astype(F32), pair_s[0, 0, 1:2].astype(F32)
@@ -126,7 +126,8 @@
         return gathered[p].at[pl.ds(pl.multiple_of(s * SHARD + lo, 16), size)]
 
     def shard_of(dx, dc):
-        return lax.rem(x + dx + RING, RING) * 2 + (1 - core if dc else core)
+        off = -dx * way if dc else dx * way
+        return lax.rem(x + off + RING, RING) * 2 + (1 - core if dc else core)
 
     started = []
 
@@ -163,10 +164,59 @@
         got(p, 7, part(p, shard_of(2, 1), 0, MID))
         got(p, 8, part(p, shard_of(2, 1), MID, MID))
 
-    own(0)
+    low = inner % 2 * MID
+    twin_low = outer % 2 * MID
+    partner = (scene, img_of(outer, inner + 1 - 2 * (inner % 2)))
+
+    def some(s, base, off, size):
+        return wa.at[pl.ds(pl.multiple_of(s * SHARD + base + off, 16), size)]
+
+    def fetched(dc, base):
+        return (
+            some(shard_of(-1, dc), base, 0, MID), some(shard_of(1, dc), base, 0, MID),
+            some(shard_of(2, dc), base, 0, 32), some(shard_of(2, dc), base, 32, 16),
+        )
+
+    ours, swapped = fetched(0, low), fetched(0, MID - low)
+    theirs = fetched(1, twin_low) + fetched(1, MID - twin_low)
+
+    def own_half():
+        half = some(scene, low, 0, MID)
+        send(0, 0, half, right)
+        send(0, 1, half, left)
+        send(0, 2, part(0, scene), twin)
+
+    def near_half():
+        got(0, 0, ours[0])
+        send(0, 3, some(shard_of(-1, 0), low, 0, 32), right)
+        send(0, 9, ours[0], partner)
+        send(0, 5, ours[0], twin)
+        got(0, 1, ours[1])
+        send(0, 4, some(shard_of(1, 0), low, 32, 16), left)
+        send(0, 10, ours[1], partner)
+        send(0, 6, ours[1], twin)
+
+    def far_half():
+        for n in (2, 3):
+            got(0, 1 + n, ours[n])
+            send(0, 9 + n, ours[n], partner)
+            send(0, 5 + n, ours[n], twin)
+
+    def swap_half():
+        for n in range(4):
+            got(0, 9 + n, swapped[n])
+            send(0, 13 + n, swapped[n], twin)
+
+    def finish_half():
+        got(0, 2, part(0, shard_of(0, 1)))
+        for n in range(4):
+            got(0, 5 + n, theirs[n])
+            got(0, 13 + n, theirs[4 + n])
+
+    own_half()
     for k in reversed(NEAR_FIRST):
-        slot = nkg.at[mypos + RING_ORDER.index(k)]
-        copy = remote(nkg.at[mypos], slot, n_send.at[0, k], n_recv.at[0, k], in_peer[k])
+        slot = nkg.at[RING_ORDER.index(k)]
+        copy = remote(nkg.at[0], slot, n_send.at[0, k], n_recv.at[0, k], in_peer[k])
         copy.start()
         started.append(copy)
     own(1)
@@ -177,13 +227,14 @@
         started.append(copy)
 
     def arrive(k):
-        slot = nkg.at[mypos + RING_ORDER.index(k)]
+        slot = nkg.at[RING_ORDER.index(k)]
         remote(slot, slot, n_send.at[0, k], n_recv.at[0, k], in_peer[k]).wait_recv()
 
     def pass_on(lo, size):
-        group = nkg.at[pl.ds(mypos + lo, size)]
+        group = nkg.at[pl.ds(lo, size)]
         for k in reversed(NEAR_FIRST):
-            remote(group, group, n_send.at[1, k], n_recv.at[1, k], out_peer[k]).start()
+            there = nkg.at[pl.ds(RING_ORDER.index(k) * SIDE + lo, size)]
+            remote(group, there, n_send.at[1, k], n_recv.at[1, k], out_peer[k]).start()
 
     for k in RING_ORDER[1:EARLY]:
         arrive(k)
@@ -202,9 +253,9 @@
         copy.start()
         started.append(copy)
     pass_on(EARLY, SIDE - EARLY)
-    near(0)
+    near_half()
     near(1)
-    far(0)
+    far_half()
 
     for k in range(1, SIDE):
         slot = turn(outer, SIDE - k)
@@ -218,10 +269,12 @@
     as_second = dot_nt(ones, jnp.where(match & (lanes >= 16) & (lanes < 32), partner, 0.0))
     pos_row = iota((IMAGES, IMAGES), 0)
     pos_col = iota((IMAGES, IMAGES), 1)
-    slot = pos_row % SIDE
-    back = (slot % 2) * ((slot + 1) // 2) + (1 - slot % 2) * (SIDE - slot // 2)
-    place = (inner - back + 2 * SIDE) % SIDE
-    image_at = (1 - core) * (pos_row // SIDE * SIDE + place) + core * (place * SIDE + pos_row // SIDE)
+    def back(slot):
+        return (slot % 2) * ((slot + 1) // 2) + (1 - slot % 2) * (SIDE - slot // 2)
+
+    at_outer = (outer - back(pos_row // SIDE) + 2 * SIDE) % SIDE
+    at_inner = (inner - back(pos_row % SIDE) + 2 * SIDE) % SIDE
+    image_at = (1 - core) * (at_outer * SIDE + at_inner) + core * (at_inner * SIDE + at_outer)
     name = (image_at + 1).astype(F32)
     m1 = jnp.sum(jnp.where(as_first[0:1] == name, 1.0, 0.0), axis=1, keepdims=True)
     m2 = jnp.sum(jnp.where(as_second[0:1] == name, 1.0, 0.0), axis=1, keepdims=True)
@@ -234,15 +287,17 @@
         jnp.where(image_at == pos_col, 1.0, 0.0), pose, (((1,), (1,)), ((), ())),
         precision=lax.Precision.HIGHEST, preferred_element_type=F32,
     )
-    mine = jnp.sum(jnp.where(iota((IMAGES, 128), 0) == mypos, pose, 0.0), axis=0, keepdims=True)
+    mine = pose[0:1]
     coef = m1 * mine + m2 * pose
     coef_s[...] = jnp.broadcast_to(coef[:, None, :], (IMAGES, TOK, 128)).reshape(IMAGES * TOK, 128)
 
-    for k in range(1, SIDE):
-        src = nkg.at[pl.ds(turn(outer, SIDE - k) * SIDE, SIDE)]
-        remote(src, src, n_send.at[1, k], n_recv.at[1, k], out_peer[k]).wait_recv()
-
-    finish(0)
+    swap_half()
+
+    def tokens_in(k, slot):
+        group = nkg.at[pl.ds(slot * SIDE, SIDE)]
+        remote(group, group, n_send.at[1, k], n_recv.at[1, k], out_peer[1]).wait_recv()
+
+    finish_half()
     q = dot(nq, wa[:, :WIDTH]).astype(BF16).astype(F32) * HEAD_DIM ** (-0.5)
     qbig = jnp.concatenate([q] * HEADS, axis=0)
     own_head = iota((HEADS * TOK, WIDTH), 0) // TOK == iota((HEADS * TOK, WIDTH), 1) // HEAD_DIM
@@ -250,6 +305,8 @@
     same = iota((ROWS, ROWS), 0) // TOK == iota((ROWS, ROWS), 1) // TOK
     head_of = iota((ROWS, WIDTH), 1) // HEAD_DIM
     x_tile = jnp.concatenate([xt] * WIDE, axis=0)
+
+    tokens_in(1, 1)
 
     def attend(g, carry):
         rows = pl.ds(pl.multiple_of(g * ROWS, ROWS), ROWS)
@@ -270,11 +327,17 @@
         split = [jnp.where(head_of == h, values, 0.0).astype(BF16) for h in range(HEADS)]
         o = dot(jnp.concatenate(spread, axis=1), jnp.concatenate(split, axis=0))
         o_s[rows] = o.astype(BF16)
+
+        @pl.when(g < IMAGES // GROUP - 1)
+        def _():
+            tokens_in(SIDE - 1 - g, 2 * g + 2)
+            tokens_in(g + 2, 2 * g + 3)
+
         return carry
 
-    lax.fori_loop(0, 2, attend, 0)
+    lax.fori_loop(0, 1, attend, 0)
     far(1)
-    lax.fori_loop(2, IMAGES // GROUP, attend, 0)
+    lax.fori_loop(1, IMAGES // GROUP, attend, 0)
     finish(1)
     for s in range(D // SHARD):
         wo[s * MID:(s + 1) * MID, :HALF] = wb[s * SHARD:s * SHARD + MID, OUT:]
@@ -329,27 +392,22 @@
             ours = ours + mine[:, 3 * k + m:3 * k + m + 1] * total[m]
         sent = jnp.where(lanes == k, m2 * theirs, sent)
         kept = jnp.where(lane == k, jnp.sum(m1 * ours, axis=0, keepdims=True), kept)
+    by_inner = [(1 - core) * turn(inner, k) + core * SIDE * turn(inner, k) for k in range(SIDE)]
     hg[...] = sent.reshape(IMAGES, 1, 128)
 
-    def give(o, k):
-        src = hg.at[o * SIDE + RING_ORDER.index((SIDE - k) % SIDE)]
-        peer = (scene, img_of(o, turn(inner, k)))
-        remote(src, hin.at[myname], g_send.at[0], g_recv.at[0], peer).start()
-
-    def give_row(n, carry):
-        u = SIDE - 1 - n
-        o = turn(outer, (u % 2) * ((u + 1) // 2) + (1 - u % 2) * (SIDE - u // 2))
+    for far_out in reversed(RING_ORDER):
+        to = turn(outer, far_out)
+        by_outer = (1 - core) * to * SIDE + core * to
+        row_of = RING_ORDER.index((SIDE - far_out) % SIDE) * SIDE
         for k in reversed(RING_ORDER):
-            give(o, k)
-        return carry
-
-    lax.fori_loop(0, SIDE - 1, give_row, 0)
-    for k in reversed(NEAR_FIRST):
-        give(outer, k)
+            if far_out == 0 and k == 0:
+                continue
+            src = hg.at[row_of + RING_ORDER.index((SIDE - k) % SIDE)]
+            remote(src, hin.at[myname], g_send.at[0], g_recv.at[0], (scene, by_outer + by_inner[k])).start()
     hin[myname] = jnp.zeros((1, 128), F32)
     for copy in started:
         copy.wait_send()
-    all_tokens = nkg.at[pl.ds(mypos, SIDE)]
+    all_tokens = nkg.at[pl.ds(0, SIDE)]
     for k in range(1, SIDE):
         remote(all_tokens, all_tokens, n_send.at[1, k], n_recv.at[1, k], out_peer[k]).wait_send()
     most = hin.at[pl.ds(0, IMAGES - 1)]
@@ -393,8 +451,8 @@
             pltpu.VMEM((IMAGES * TOK, 128), F32),
             pltpu.VMEM((IMAGES, 1, 128), F32),
             pltpu.VMEM((IMAGES, 1, 128), F32),
-            dma((2, 9)),
-            dma((2, 9)),
+            dma((2, 17)),
+            dma((2, 17)),
             dma((2, SIDE)),
             dma((2, SIDE)),
             dma((2, SIDE)),

time: 50.5 us -> 49.8 us (0.986)
  Pallas kernels: 47.2 us -> 46.5 us
    pallas_call x1, Pallas kernels: 47.2 us -> 46.5 us  [on_device(): pl.pallas_call(kernel, out_shape=(jax.ShapeDtypeStruct((1, 1, 3, TOK * PI...]
where the time goes in v4:
time: 49.8 us; the launch traced here: 49.6 us
  Pallas kernels  46.5 us (93%)
  local copies, waits for them, and re-layouts  1.84 us (4%)
  between operations  1.3 us (3%)
    pallas_call x1, Pallas kernels, on_device(): pl.pallas_call(kernel, out_shape=(jax.ShapeDtypeStruct((1, 1, 3, TOK * PI...  46.5 us
    unnamed x4, local copies, waits for them, and re-layouts  1.84 us

profile of v4, /device:TPU:1, one launch (start us, length us, event | category | flops | bytes accessed | tf_op | source)
XLA Modules:
  0.0 49.6 jit_solution(12861337463141770329)
XLA Ops:
  1.3 46.5 %shard_map.113 = (bf16[1,1,3,2048]{3,2,1,0:T(4,128)(2,1)}, f32[1,1,3]{2,1,0:T(1,128)}) custom-call(bf16[1,1,8,768]{3,2,1,0:T(8,128)(2,1)} %tok_in.1, s32[1,1,2,16]{3,2,1,0:T(2,128)} %bitcast.3, s32[1,1]{1,0:T(1,128)S(6)} %copy.14.count_in, f32[12,1,64]{2,1,0:T(1,128)} %bitcast.2, f32[768]{0:T(1024)} %gq_in.1, f32[768]{0:T(1024)} %gk_in.1, ...), custom_call_target="tpu_custom_call" | custom-call | tf_op jit(solution)/shard_map/pallas_call | solution.py:427
  47.8 0.0 copy-start
  47.8 1.3 %copy.15 = bf16[1,1,3,2048]{3,2,1,0:T(4,128)(2,1)} copy(bf16[1,1,3,2048]{3,2,1,0:T(4,128)(2,1)} %get-tuple-element.4) | data formatting | bytes 24576
  49.1 0.0 copy-done
  49.1 0.5 %copy.16 = f32[1,1,3]{2,1,0:T(1,128)} copy(f32[1,1,3]{2,1,0:T(1,128)S(1)} %copy-done) | data formatting | bytes 24
Async XLA Ops:
  47.8 1.3 %copy-start = (f32[1,1,3]{2,1,0:T(1,128)S(1)}, f32[1,1,3]{2,1,0:T(1,128)}, u32[]{:S(2)}) copy-start(f32[1,1,3]{2,1,0:T(1,128)} %get-tuple-element.5) | copy-start | bytes 40

commit v5 on v4

--- a/solution.py
+++ b/solution.py
@@ -213,12 +213,12 @@
             got(0, 5 + n, theirs[n])
             got(0, 13 + n, theirs[4 + n])
 
-    own_half()
     for k in reversed(NEAR_FIRST):
         slot = nkg.at[RING_ORDER.index(k)]
         copy = remote(nkg.at[0], slot, n_send.at[0, k], n_recv.at[0, k], in_peer[k])
         copy.start()
         started.append(copy)
+    own_half()
     own(1)
     for k in reversed(NEAR_FIRST):
         slot = info_in.at[inner]
@@ -335,9 +335,8 @@
 
         return carry
 
-    lax.fori_loop(0, 1, attend, 0)
     far(1)
-    lax.fori_loop(1, IMAGES // GROUP, attend, 0)
+    lax.fori_loop(0, IMAGES // GROUP, attend, 0)
     finish(1)
     for s in range(D // SHARD):
         wo[s * MID:(s + 1) * MID, :HALF] = wb[s * SHARD:s * SHARD + MID, OUT:]

time: 49.8 us -> 49.8 us (level)
  no operation moved by 1% of the time
where the time goes in v5:
time: 49.8 us; the launch traced here: 49.6 us
  Pallas kernels  46.5 us (93%)
  local copies, waits for them, and re-layouts  1.84 us (4%)
  between operations  1.3 us (3%)
    pallas_call x1, Pallas kernels, on_device(): pl.pallas_call(kernel, out_shape=(jax.ShapeDtypeStruct((1, 1, 3, TOK * PI...  46.5 us
    unnamed x4, local copies, waits for them, and re-layouts  1.84 us

profile of v5, /device:TPU:1, one launch (start us, length us, event | category | flops | bytes accessed | tf_op | source)
XLA Modules:
  0.0 49.6 jit_solution(4519828094292533148)
XLA Ops:
  1.3 46.5 %shard_map.113 = (bf16[1,1,3,2048]{3,2,1,0:T(4,128)(2,1)}, f32[1,1,3]{2,1,0:T(1,128)}) custom-call(bf16[1,1,8,768]{3,2,1,0:T(8,128)(2,1)} %tok_in.1, s32[1,1,2,16]{3,2,1,0:T(2,128)} %bitcast.3, s32[1,1]{1,0:T(1,128)S(6)} %copy.14.count_in, f32[12,1,64]{2,1,0:T(1,128)} %bitcast.2, f32[768]{0:T(1024)} %gq_in.1, f32[768]{0:T(1024)} %gk_in.1, ...), custom_call_target="tpu_custom_call" | custom-call | tf_op jit(solution)/shard_map/pallas_call | solution.py:426
  47.8 0.0 copy-start
  47.8 1.3 %copy.15 = bf16[1,1,3,2048]{3,2,1,0:T(4,128)(2,1)} copy(bf16[1,1,3,2048]{3,2,1,0:T(4,128)(2,1)} %get-tuple-element.4) | data formatting | bytes 24576
  49.1 0.0 copy-done
  49.1 0.5 %copy.16 = f32[1,1,3]{2,1,0:T(1,128)} copy(f32[1,1,3]{2,1,0:T(1,128)S(1)} %copy-done) | data formatting | bytes 24
Async XLA Ops:
  47.8 1.3 %copy-start = (f32[1,1,3]{2,1,0:T(1,128)S(1)}, f32[1,1,3]{2,1,0:T(1,128)}, u32[]{:S(2)}) copy-start(f32[1,1,3]{2,1,0:T(1,128)} %get-tuple-element.5) | copy-start | bytes 40
